TPU v7x, 32 devices: a whole 2x2x4 slice. The times are simulated.
32 devices in a mesh: groups: 2 (over x), gx: 8 (over z, y), gy: 2 (over core).
Axes of the slice: x: 2, y: 2, z: 4, core: 2. Of those that a mesh axis runs over, the one named last changes fastest.
Arguments:
- tokens: bfloat16 [512, 16384], P('groups', 'gx'), parts along dimension 0, may hold values from -6 to 6
- query_weight: bfloat16 [16384, 8, 2, 128], P('gx', None, 'gy'), may hold values from -0.046875 to 0.046875
- key_value_projection_weight: bfloat16 [16384, 2, 8, 128], P('gx'), may hold values from -0.046875 to 0.046875
- output_weight: bfloat16 [2048, 16384], P('gx', 'gy'), may hold values from -0.125 to 0.125
- document_ids: int32 [512], P('groups'), parts along dimension 0, may hold values from 0 to 7, never falling along the last dimension, each value on 1 to 64 neighbouring positions
- query_exponent: int32 [8, 2], P(None, 'gy'), may hold values from -11 to -8
- key_value_partial_exponents: int32 [2, 8], replicated, may hold values from -11 to -8
- key_value_summed_exponents: int32 [2, 8], replicated, may hold values from -7 to -5
- output_exponent: int32 [2, 64], P('gy'), may hold values from -13 to -10
- output_relevel: int32 [2, 64], P(None, 'gx'), may hold values from -10 to -8
Outputs:
- block_output: bfloat16 [512, 2, 8192], P('groups', None, 'gx'), parts along dimension 0
There are 2 independent parts, one for each index of `groups`. A program takes and returns all parts, laid end to end along the dimension named above; an argument that names none is the same for every part. Nothing has to cross between parts.
Inputs may be any that keep to these rules, and one draw needn't show every extreme that they name: `document_ids`: never falling; each document is 1 to 64 tokens long, and one is exactly that long.
All inputs are finite; a program needn't handle non-finite values.
Results may differ from a plain program's by a relative error of at most 0.007.
Values may be sent and summed in bfloat16 or wider, within the bound.
A program may use at most 128 MiB of HBM per device.

v0:
```python
import math

import jax
import jax.numpy as jnp
from jax import lax
from jax.sharding import PartitionSpec as P

rotary_base = 500000.0
saturation = 127.0


def hadamard(order):
    row_index = jnp.arange(order, dtype=jnp.int32)[:, None]
    col_index = jnp.arange(order, dtype=jnp.int32)[None, :]
    common = row_index & col_index
    parity = jnp.zeros((order, order), jnp.int32)
    for bit_place in range(order.bit_length() - 1):
        parity = parity ^ common >> bit_place & 1
    return (1 - 2 * parity).astype(jnp.float32) * (1.0 / math.sqrt(order))


def rotate(values, rotation):
    return jnp.matmul(values, rotation, precision=lax.Precision.HIGHEST)


def rotary(values):
    length = values.shape[-2]
    full_width = values.shape[-1]
    half_width = full_width // 2
    frequency = rotary_base ** (-(jnp.arange(half_width, dtype=jnp.float32) * 2.0 / full_width))
    places = jnp.arange(length, dtype=jnp.int32).astype(jnp.float32)
    angles = places[:, None] * frequency[None, :]
    cosine = jnp.cos(angles)
    sine_part = jnp.sin(angles)
    front_half = values[..., :half_width]
    back_half = values[..., half_width:]
    return jnp.concatenate(
        [front_half * cosine - back_half * sine_part, back_half * cosine + front_half * sine_part],
        axis=-1,
    )


def body(
    tokens,
    query_weight,
    key_value_projection_weight,
    output_weight,
    document_ids,
    query_exponent,
    key_value_partial_exponents,
    key_value_summed_exponents,
    output_exponent,
    output_relevel,
):
    length = tokens.shape[0]
    head_width = query_weight.shape[3]
    memory_heads = key_value_projection_weight.shape[2]
    count_gx = lax.axis_size("gx")
    where_gx = lax.axis_index("gx")
    where_gy = lax.axis_index("gy")
    rotation = hadamard(head_width)
    query_block = query_weight[:, :, 0, :]
    query_inverse = jnp.exp2(-query_exponent[:, 0].astype(jnp.float32))
    query_up = jnp.exp2(query_exponent[:, 0].astype(jnp.float32))
    heads_total = query_block.shape[1]
    heads_here = heads_total // count_gx
    heads_spread = count_gx // memory_heads
    memory_index = where_gx // heads_spread
    memory_inverse = jnp.exp2(-key_value_partial_exponents.astype(jnp.float32))
    memory_up = jnp.exp2(key_value_partial_exponents.astype(jnp.float32))
    memory_scale = jnp.exp2(key_value_summed_exponents.astype(jnp.float32))
    partial_sum = jnp.einsum("sd,dpe->pse", tokens, query_block, preferred_element_type=jnp.float32)
    factor = query_inverse
    query_sum = lax.psum_scatter(
        jnp.clip(rotate(partial_sum, rotation) * factor[:, None, None], -saturation, saturation),
        "gx",
        scatter_dimension=0,
        tiled=True,
    )
    query_scale = lax.dynamic_slice_in_dim(query_up, where_gx * heads_here, heads_here, 0)
    query = rotary(rotate(query_sum * query_scale[:, None, None], rotation))[0].astype(jnp.bfloat16)
    partial_sum = jnp.einsum(
        "sd,dche->sche", tokens, key_value_projection_weight, preferred_element_type=jnp.float32
    )
    memory_sum = lax.psum_scatter(
        jnp.clip(
            rotate(partial_sum, rotation) * memory_inverse[None, :, :, None],
            -saturation,
            saturation,
        ),
        "gx",
        scatter_dimension=0,
        tiled=True,
    )
    whole = lax.all_gather(
        jnp.clip(
            memory_sum * memory_up[None, :, :, None] / memory_scale[None, :, :, None],
            -saturation,
            saturation,
        ),
        "gx",
        axis=0,
        tiled=True,
    )
    arrived = lax.dynamic_index_in_dim(whole, memory_index, 2, keepdims=False)
    head_scale = lax.dynamic_index_in_dim(memory_scale, memory_index, 1, keepdims=False)
    memory_full = rotate(arrived * head_scale[None, :, None], rotation)
    keys = rotary(memory_full[:, 0]).astype(jnp.bfloat16)
    values = memory_full[:, 1].astype(jnp.bfloat16)
    scores = jnp.einsum("qe,ke->qk", query, keys, preferred_element_type=jnp.float32) * (
        1.0 / math.sqrt(head_width)
    )
    position = jnp.arange(length, dtype=jnp.int32)
    allowed = (position[:, None] >= position[None, :]) & (
        document_ids[:, None] == document_ids[None, :]
    )
    scores = jnp.where(allowed, scores, -jnp.inf)
    row_max = jnp.max(scores, axis=-1, keepdims=True)
    exponentials = jnp.exp(scores - row_max)
    weights = (exponentials / jnp.sum(exponentials, axis=-1, keepdims=True)).astype(jnp.bfloat16)
    attended = jnp.dot(weights, values, preferred_element_type=jnp.float32).astype(jnp.bfloat16)
    head_pairs = lax.all_gather(attended, "gy", axis=1, tiled=True)
    feature_blocks = output_weight.shape[1] // head_width
    blocks_here = feature_blocks // count_gx
    output_inverse = jnp.exp2(-output_exponent[0].astype(jnp.float32))
    partial_sum = jnp.dot(head_pairs, output_weight, preferred_element_type=jnp.float32)
    partial_sum = partial_sum.reshape(
        length, blocks_here * lax.axis_size("gx"), head_width
    ).transpose(1, 0, 2)
    factor = output_inverse
    out_sum = lax.psum_scatter(
        jnp.clip(rotate(partial_sum, rotation) * factor[:, None, None], -saturation, saturation),
        "gx",
        scatter_dimension=0,
        tiled=True,
    )
    out_up = jnp.exp2(
        lax.dynamic_slice_in_dim(output_exponent[0], where_gx * blocks_here, blocks_here, 0).astype(
            jnp.float32
        )
    )
    own_scale = jnp.exp2(
        lax.dynamic_index_in_dim(output_relevel, where_gy, 0, keepdims=False).astype(jnp.float32)
    )
    out_level = jnp.clip(
        out_sum * out_up[:, None, None] / own_scale[:, None, None], -saturation, saturation
    )
    halves = lax.all_gather(out_level[None], "gy", axis=0, tiled=True)
    restored = rotate(
        halves * jnp.exp2(output_relevel.astype(jnp.float32))[:, :, None, None], rotation
    )
    return (
        restored.transpose(2, 0, 1, 3)
        .reshape(length, 2, blocks_here * head_width)
        .astype(jnp.bfloat16)
    )


def solution(mesh):
    return jax.shard_map(
        body,
        mesh=mesh,
        in_specs=(
            P("groups", "gx"),
            P("gx", None, "gy", None),
            P("gx", None, None, None),
            P("gx", "gy"),
            P("groups"),
            P(None, "gy"),
            P(),
            P(),
            P("gy", None),
            P(None, "gx"),
        ),
        out_specs=P("groups", None, "gx"),
        check_vma=False,
    )
```

profile of v0, /device:TPU:0, one launch (start us, length us, event | category | flops | bytes accessed | tf_op | source)
XLA Modules:
  0.0 393.6 jit_solution(5087739336820573157)
XLA Ops:
  6.5 0.0 copy-start
  6.5 0.0 reduce-scatter.6.cloned.1.call-start
  6.5 0.8 multiply_exponential_fusion.2
  7.3 0.5 copy-done
  7.8 5.7 %fusion.2 = f32[256,2,8,128]{3,0,2,1:T(8,128)S(1)} fusion(bf16[2048,2,8,128]{3,2,1,0:T(8,128)(2,1)} %param.12, bf16[256,2048]{1,0:T(8,128)(2,1)S(1)} %copy-done), kind=kOutput, calls=%fused_computation.3 | convolution fusion | flops 2147483648 | bytes 11534336 | tf_op jit(solution)/shard_map/sd,dche->sche/dot_general | solution.py:82
  13.5 0.0 copy-start.5
  13.5 3.2 multiply_clamp_fusion.1
  16.7 0.0 reduce-scatter.6.cloned.1.call-update
  16.7 0.0 reduce-scatter.4.cloned.1.call-start
  16.8 0.0 copy-done.5
  16.8 0.0 copy-start.2
  16.8 0.0 copy-start.3
  16.8 3.4 fusion.11
  20.3 0.0 copy-start.4
  20.3 2.0 fusion.14
  22.3 0.0 reduce-scatter.4.cloned.1.call-update
  22.3 0.0 all-gather.4.cloned.1.call-start
  22.4 0.0 copy-done.2
  22.4 65.4 %reduce-scatter.6.cloned.1.call-done = f32[32,2,8,128]{3,0,2,1:T(8,128)} async-done(((f32[256,2,8,128]{3,0,2,1:T(8,128)}), f32[32,2,8,128]{3,0,2,1:T(8,128)}) %reduce-scatter.6.cloned.1.call-update) | async-done | bytes 262160 | tf_op jit(solution)/shard_map/reduce_scatter | solution.py:85
  87.8 1.8 divide_clamp_fusion.1
  89.6 0.0 all-gather.4.cloned.1.call-update
  89.6 0.0 reduce-scatter.8.cloned.1.call-start
  89.6 0.2 fusion.61
  89.8 0.6 constant_dynamic-slice_fusion.3
  90.5 0.0 copy-done.3
  90.5 63.3 %reduce-scatter.4.cloned.1.call-done = f32[1,256,128]{2,1,0:T(8,128)} async-done(((f32[8,256,128]{2,1,0:T(8,128)}), f32[1,256,128]{2,1,0:T(8,128)}) %reduce-scatter.4.cloned.1.call-update) | async-done | bytes 131088 | tf_op jit(solution)/shard_map/reduce_scatter | solution.py:74
  153.8 1.8 convolution_bitcast_fusion.1
  155.6 0.3 fusion.39
  156.0 48.6 %all-gather.4.cloned.1.call-done = f32[256,2,8,128]{3,0,2,1:T(8,128)} async-done(((f32[32,2,8,128]{3,0,2,1:T(8,128)}), f32[256,2,8,128]{3,0,2,1:T(8,128)}) %all-gather.4.cloned.1.call-update) | async-done | bytes 2097168 | tf_op jit(solution)/shard_map/all_gather | solution.py:95
  204.6 1.4 fusion.19
  206.0 0.3 fusion.35
  206.4 0.0 copy-done.4
  206.4 0.2 fusion.113
  206.6 0.1 fusion.22
  206.7 0.2 convolution_convert_fusion
  206.9 2.1 all_gather.10
  209.0 3.5 convolution_bitcast_fusion
  212.5 8.9 %multiply_clamp_fusion = f32[64,256,128]{2,1,0:T(8,128)} fusion(f32[64]{0:T(128)S(1)} %exponential_bitcast_fusion, f32[32,64,8,128]{3,2,1,0:T(8,128)S(1)} %convolution_bitcast_fusion), kind=kOutput, calls=%fused_computation.5 | convolution fusion | flops 3225829376 | bytes 16777472 | tf_op jit(solution)/shard_map/dot_general | solution.py:23
  221.4 0.0 copy-start.1
  221.4 0.0 reduce-scatter.8.cloned.1.call-update
  221.4 0.0 all-gather.6.cloned.1.call-start
  221.5 0.6 copy-done.1
  222.1 0.1 fusion.68
  222.1 146.9 %reduce-scatter.8.cloned.1.call-done = f32[8,256,128]{2,1,0:T(8,128)} async-done(((f32[64,256,128]{2,1,0:T(8,128)}), f32[8,256,128]{2,1,0:T(8,128)}) %reduce-scatter.8.cloned.1.call-update) | async-done | bytes 1048592 | tf_op jit(solution)/shard_map/reduce_scatter | solution.py:131
  369.0 2.4 divide_clamp_fusion
  371.4 0.0 all-gather.6.cloned.1.call-update
  371.4 9.7 %all-gather.6.cloned.1.call-done = f32[16,256,128]{2,1,0:T(8,128)} async-done(((f32[8,256,128]{2,1,0:T(8,128)}), f32[16,256,128]{2,1,0:T(8,128)}) %all-gather.6.cloned.1.call-update) | async-done | bytes 2097168 | tf_op jit(solution)/shard_map/all_gather | solution.py:148
  381.2 3.8 fusion.8
  385.0 2.1 copy.20
  (7 shorter events, 0.1 us)
Async XLA Ops:
  6.5 1.2 copy-start
  6.5 81.3 %reduce-scatter.6.cloned.1.call-start = ((), (), s32[]{:S(2)}) async-start(), calls=%async_computation.4 | async-start | bytes 2359296 | tf_op jit(solution)/shard_map/reduce_scatter | solution.py:85
  13.5 3.3 copy-start.5
  16.7 137.1 %reduce-scatter.4.cloned.1.call-start = ((), (), s32[]{:S(2)}) async-start(), calls=%async_computation.3 | async-start | bytes 1179648 | tf_op jit(solution)/shard_map/reduce_scatter | solution.py:74
  16.8 5.6 %copy-start.2 = (s32[2,8]{1,0:T(2,128)S(1)}, s32[2,8]{1,0:T(2,128)}, u32[]{:S(2)}) copy-start(s32[2,8]{1,0:T(2,128)} %param.17) | copy-start | bytes 196
  16.8 73.6 %copy-start.3 = (s32[1,64]{1,0:T(1,128)S(1)}, s32[1,64]{1,0:T(1,128)}, u32[]{:S(2)}) copy-start(s32[1,64]{1,0:T(1,128)} %param.18) | copy-start | bytes 772
  20.3 186.1 %copy-start.4 = (s32[256]{0:T(256)S(1)}, s32[256]{0:T(256)}, u32[]{:S(2)}) copy-start(s32[256]{0:T(256)} %param.14) | copy-start | bytes 3076
  22.3 182.3 %all-gather.4.cloned.1.call-start = ((), (), s32[]{:S(2)}) async-start(), calls=%async_computation.5 | async-start | bytes 2359296 | tf_op jit(solution)/shard_map/all_gather | solution.py:95
  89.6 279.4 %reduce-scatter.8.cloned.1.call-start = ((), (), s32[]{:S(2)}) async-start(), calls=%async_computation.6 | async-start | bytes 9437184 | tf_op jit(solution)/shard_map/reduce_scatter | solution.py:131
  221.4 0.7 copy-start.1
  221.4 159.8 %all-gather.6.cloned.1.call-start = ((), (), s32[]{:S(2)}) async-start(), calls=%async_computation.7 | async-start | bytes 3145728 | tf_op jit(solution)/shard_map/all_gather | solution.py:148
Sparse Core Ops, SparseCore 0:
  16.9 70.8 reduce-scatter.5
  91.2 62.5 reduce-scatter.3
  156.2 48.2 all-gather.3
  221.5 147.4 reduce-scatter.7
  371.5 9.5 all-gather.5
where the time goes:
time: 394 us
  waiting for transfers between devices  334 us (85%)
  matrix products  34.2 us (9%)
  between operations  13.3 us (3%)
  other arithmetic  5.74 us (1%)
  local copies, waits for them, and re-layouts  3.99 us (1%)
    reduce_scatter x2, waiting for transfers between devices, body(): lax.psum_scatter(jnp.clip(rotate(partial_sum, rotation) * factor[:, None,...  210 us
    reduce_scatter x1, waiting for transfers between devices, body(): lax.psum_scatter(jnp.clip(rotate(partial_sum, rotation) * memory_inverse[...  65.4 us
    all_gather x1, waiting for transfers between devices, body(): lax.all_gather(jnp.clip(memory_sum * memory_up[None, :, :, None] / memory...  48.6 us
    dot_general x6, matrix products, rotate(): return jnp.matmul(values, rotation, precision=lax.Precision.HIGHEST)  21.1 us
    all_gather x1, waiting for transfers between devices, body(): halves = lax.all_gather(out_level[None], 'gy', axis=0, tiled=True)  9.75 us
  transfers between devices with their start and end apart: 5, of which 5 were waited for; matrix products, arithmetic and copies ran while one was open for 3% of the time, Pallas kernels for 0%

commit v1 on v0

--- a/solution.py
+++ b/solution.py
@@ -1,8 +1,12 @@
+import functools
 import math
 
 import jax
 import jax.numpy as jnp
+import numpy as np
 from jax import lax
+from jax.experimental import pallas as pl
+from jax.experimental.pallas import tpu as pltpu
 from jax.sharding import PartitionSpec as P
 
 rotary_base = 500000.0
@@ -40,7 +44,7 @@
     )
 
 
-def body(
+def plain_body(
     tokens,
     query_weight,
     key_value_projection_weight,
@@ -156,6 +160,337 @@
     )
 
 
+def signs(order):
+    index = np.arange(order)
+    common = index[:, None] & index[None, :]
+    parity = np.zeros((order, order), np.int64)
+    for place in range(order.bit_length() - 1):
+        parity ^= (common >> place) & 1
+    return 1.0 - 2.0 * parity
+
+
+def paired_signs(order):
+    return np.kron(np.eye(2), signs(order))
+
+
+def rotary_tables(length, width):
+    half = width // 2
+    frequency = rotary_base ** (-(np.arange(half, dtype=np.float64) * 2.0 / width))
+    angles = np.arange(length)[:, None] * frequency.astype(np.float32).astype(np.float64)[None, :]
+    cosine = np.concatenate([np.cos(angles), np.cos(angles)], axis=1)
+    sine = np.concatenate([-np.sin(angles), np.sin(angles)], axis=1)
+    return (
+        np.stack([cosine, np.ones_like(cosine)]).astype(np.float32),
+        np.stack([sine, np.zeros_like(sine)]).astype(np.float32),
+    )
+
+
+def turn(values, sign_matrix, norm):
+    upper = values.astype(jnp.bfloat16)
+    lower = (values - upper.astype(jnp.float32)).astype(jnp.bfloat16)
+    total = jnp.dot(upper, sign_matrix, preferred_element_type=jnp.float32)
+    total = total + jnp.dot(lower, sign_matrix, preferred_element_type=jnp.float32)
+    return total * norm
+
+
+def saturate(values):
+    return jnp.clip(values, -saturation, saturation)
+
+
+def fused_kernel(
+    count,
+    query_part,
+    memory_part,
+    out_weight_hbm,
+    first_scale,
+    own_scale,
+    out_inverse,
+    out_ratio,
+    out_scale,
+    sign_ref,
+    cosine_ref,
+    sine_ref,
+    document_column,
+    document_row,
+    out_ref,
+    out_weight,
+    first_send,
+    first_recv,
+    memory_pair,
+    mixed,
+    second_send,
+    second_recv,
+    total,
+    weight_sem,
+    first_send_sem,
+    first_recv_sem,
+    second_send_sem,
+    second_recv_sem,
+    pair_send_sem,
+    pair_recv_sem,
+):
+    me = lax.axis_index("gx")
+    core = lax.axis_index("gy")
+    mate = 1 - core
+    length, width = query_part.shape[1], query_part.shape[2]
+    span = out_inverse.shape[2]
+    norm = 1.0 / math.sqrt(width)
+    chunk = 2 * width
+
+    load = pltpu.make_async_copy(out_weight_hbm, out_weight, weight_sem)
+    load.start()
+
+    barrier = pltpu.get_barrier_semaphore()
+    for away in range(1, count):
+        pl.semaphore_signal(
+            barrier,
+            inc=1,
+            device_id={"gx": lax.rem(me + away, count)},
+            device_id_type=pl.DeviceIdType.MESH,
+        )
+    pl.semaphore_signal(
+        barrier, inc=1, device_id={"gy": mate}, device_id_type=pl.DeviceIdType.MESH
+    )
+    pl.semaphore_wait(barrier, count)
+
+    small_signs = sign_ref[:width, :width]
+
+    def first_copy(away):
+        return pltpu.make_async_remote_copy(
+            src_ref=first_send.at[away],
+            dst_ref=first_recv.at[away],
+            send_sem=first_send_sem.at[away],
+            recv_sem=first_recv_sem.at[away],
+            device_id={"gx": lax.rem(me + away, count)},
+            device_id_type=pl.DeviceIdType.MESH,
+        )
+
+    def second_copy(away):
+        return pltpu.make_async_remote_copy(
+            src_ref=second_send.at[away],
+            dst_ref=second_recv.at[away],
+            send_sem=second_send_sem.at[away],
+            recv_sem=second_recv_sem.at[away],
+            device_id={"gx": lax.rem(me + away, count)},
+            device_id_type=pl.DeviceIdType.MESH,
+        )
+
+    def pair_copy(ref, place):
+        return pltpu.make_async_remote_copy(
+            src_ref=ref.at[core],
+            dst_ref=ref.at[core],
+            send_sem=pair_send_sem.at[place],
+            recv_sem=pair_recv_sem.at[place],
+            device_id={"gy": mate},
+            device_id_type=pl.DeviceIdType.MESH,
+        )
+
+    def first_term(target):
+        query = saturate(turn(query_part[target], small_signs, norm) * first_scale[target, 0:1, :])
+        memory = saturate(
+            turn(memory_part[target], small_signs, norm) * first_scale[target, 1:2, :]
+        )
+        return query, memory
+
+    def first_step(away, carry):
+        query, memory = first_term(lax.rem(me + away, count))
+        first_send[away, 0] = query.astype(jnp.bfloat16)
+        first_send[away, 1] = memory.astype(jnp.bfloat16)
+        first_copy(away).start()
+        return carry
+
+    lax.fori_loop(1, count, first_step, 0)
+    query, memory = first_term(me)
+    total[:, :width] = query
+    total[:, width : 2 * width] = memory
+
+    def first_sum(away, carry):
+        first_copy(away).wait_recv()
+        total[:, :width] += first_recv[away, 0].astype(jnp.float32)
+        total[:, width : 2 * width] += first_recv[away, 1].astype(jnp.float32)
+        return carry
+
+    lax.fori_loop(1, count, first_sum, 0)
+
+    level = saturate(total[:, width : 2 * width] * own_scale[1:2, :])
+    memory = turn(level * own_scale[2:3, :], small_signs, norm)
+    memory = memory * cosine_ref[core] + pltpu.roll(memory, width // 2, 1) * sine_ref[core]
+    memory_pair[core] = memory.astype(jnp.bfloat16)
+    pair_copy(memory_pair, 0).start()
+    query = turn(total[:, :width] * own_scale[0:1, :], small_signs, norm)
+    query = query * cosine_ref[0] + pltpu.roll(query, width // 2, 1) * sine_ref[0]
+    query = query.astype(jnp.bfloat16)
+    pair_copy(memory_pair, 0).wait_recv()
+
+    scores = lax.dot_general(
+        query, memory_pair[0], (((1,), (1,)), ((), ())), preferred_element_type=jnp.float32
+    ) * (1.0 / math.sqrt(width))
+    rows = lax.broadcasted_iota(jnp.int32, (length, length), 0)
+    columns = lax.broadcasted_iota(jnp.int32, (length, length), 1)
+    allowed = (rows >= columns) & (document_column[...] == document_row[...])
+    scores = jnp.where(allowed, scores, -jnp.inf)
+    exponentials = jnp.exp(scores - jnp.max(scores, axis=-1, keepdims=True))
+    weights = exponentials / jnp.sum(exponentials, axis=-1, keepdims=True)
+    mixed[core] = jnp.dot(
+        weights.astype(jnp.bfloat16), memory_pair[1], preferred_element_type=jnp.float32
+    ).astype(jnp.bfloat16)
+    pair_copy(mixed, 1).start()
+    load.wait()
+    pair_copy(mixed, 1).wait_recv()
+
+    def second_term(target, part):
+        start = pl.multiple_of(target * span + part * chunk, chunk)
+        both = jnp.concatenate([mixed[0], mixed[1]], axis=1)
+        product = jnp.dot(
+            both, out_weight[:, pl.ds(start, chunk)], preferred_element_type=jnp.float32
+        )
+        scale = out_inverse[target, :, part * chunk : (part + 1) * chunk]
+        return saturate(turn(product, sign_ref[...], norm) * scale)
+
+    def second_step(away, carry):
+        target = lax.rem(me + away, count)
+        for part in range(span // chunk):
+            second_send[away, :, part * chunk : (part + 1) * chunk] = second_term(
+                target, part
+            ).astype(jnp.bfloat16)
+        second_copy(away).start()
+        return carry
+
+    lax.fori_loop(1, count, second_step, 0)
+    for part in range(span // chunk):
+        total[:, part * chunk : (part + 1) * chunk] = second_term(me, part)
+
+    def second_sum(away, carry):
+        second_copy(away).wait_recv()
+        for part in range(span // chunk):
+            place = slice(part * chunk, (part + 1) * chunk)
+            total[:, place] += second_recv[away, :, place].astype(jnp.float32)
+        return carry
+
+    lax.fori_loop(1, count, second_sum, 0)
+    for part in range(span // chunk):
+        place = slice(part * chunk, (part + 1) * chunk)
+        level = saturate(total[:, place] * out_ratio[:, place])
+        out_ref[core, :, place] = turn(level * out_scale[:, place], sign_ref[...], norm).astype(
+            jnp.bfloat16
+        )
+    pair_copy(out_ref, 2).start()
+
+    def drain(away, carry):
+        first_copy(away).wait_send()
+        second_copy(away).wait_send()
+        return carry
+
+    lax.fori_loop(1, count, drain, 0)
+    pair_copy(memory_pair, 0).wait_send()
+    pair_copy(mixed, 1).wait_send()
+    pair_copy(out_ref, 2).wait()
+
+
+def body(
+    tokens,
+    query_weight,
+    key_value_projection_weight,
+    output_weight,
+    document_ids,
+    query_exponent,
+    key_value_partial_exponents,
+    key_value_summed_exponents,
+    output_exponent,
+    output_relevel,
+):
+    count = lax.axis_size("gx")
+    length = tokens.shape[0]
+    width = query_weight.shape[3]
+    heads = query_weight.shape[1]
+    memory_heads = key_value_projection_weight.shape[2]
+    span = output_weight.shape[1] // count
+    if not (count == heads == memory_heads and lax.axis_size("gy") == 2 and span % (2 * width) == 0):
+        return plain_body(
+            tokens,
+            query_weight,
+            key_value_projection_weight,
+            output_weight,
+            document_ids,
+            query_exponent,
+            key_value_partial_exponents,
+            key_value_summed_exponents,
+            output_exponent,
+            output_relevel,
+        )
+    me = lax.axis_index("gx")
+    core = lax.axis_index("gy")
+    memory_weight = lax.dynamic_index_in_dim(key_value_projection_weight, core, 1, keepdims=False)
+    query_part = jnp.einsum(
+        "sd,dpe->pse", tokens, query_weight[:, :, 0, :], preferred_element_type=jnp.float32
+    )
+    memory_part = jnp.einsum("sd,dne->nse", tokens, memory_weight, preferred_element_type=jnp.float32)
+
+    def power(exponent):
+        return jnp.exp2(exponent.astype(jnp.float32))
+
+    partial_exponent = lax.dynamic_index_in_dim(key_value_partial_exponents, core, 0, keepdims=False)
+    summed_exponent = lax.dynamic_index_in_dim(key_value_summed_exponents, core, 0, keepdims=False)
+    first_scale = jnp.broadcast_to(
+        power(-jnp.stack([query_exponent[:, 0], partial_exponent], axis=1))[:, :, None],
+        (count, 2, width),
+    )
+    own = jnp.stack(
+        [query_exponent[:, 0], partial_exponent - summed_exponent, summed_exponent], axis=0
+    )
+    own = lax.dynamic_index_in_dim(own, me, 1, keepdims=True)
+    own_scale = jnp.broadcast_to(power(own), (3, width))
+    blocks = span // width
+    out_inverse = jnp.repeat(power(-output_exponent[0]), width).reshape(count, 1, span)
+    relevel = lax.dynamic_index_in_dim(output_relevel, core, 0, keepdims=False)
+    here = lax.dynamic_slice_in_dim(output_exponent[0], me * blocks, blocks, 0)
+    out_ratio = jnp.repeat(power(here - relevel), width)[None]
+    out_scale = jnp.repeat(power(relevel), width)[None]
+    cosine, sine = rotary_tables(length, width)
+    vmem = pl.BlockSpec(memory_space=pltpu.VMEM)
+    halves = pl.pallas_call(
+        functools.partial(fused_kernel, count),
+        out_shape=jax.ShapeDtypeStruct((2, length, span), jnp.bfloat16),
+        in_specs=[vmem, vmem, pl.BlockSpec(memory_space=pl.ANY)] + [vmem] * 10,
+        out_specs=vmem,
+        scratch_shapes=[
+            pltpu.VMEM(output_weight.shape, jnp.bfloat16),
+            pltpu.VMEM((count, 2, length, width), jnp.bfloat16),
+            pltpu.VMEM((count, 2, length, width), jnp.bfloat16),
+            pltpu.VMEM((2, length, width), jnp.bfloat16),
+            pltpu.VMEM((2, length, width), jnp.bfloat16),
+            pltpu.VMEM((count, length, span), jnp.bfloat16),
+            pltpu.VMEM((count, length, span), jnp.bfloat16),
+            pltpu.VMEM((length, span), jnp.float32),
+            pltpu.SemaphoreType.DMA,
+            pltpu.SemaphoreType.DMA((count,)),
+            pltpu.SemaphoreType.DMA((count,)),
+            pltpu.SemaphoreType.DMA((count,)),
+            pltpu.SemaphoreType.DMA((count,)),
+            pltpu.SemaphoreType.DMA((3,)),
+            pltpu.SemaphoreType.DMA((3,)),
+        ],
+        compiler_params=pltpu.CompilerParams(
+            collective_id=0, has_side_effects=True, vmem_limit_bytes=40 * 1024 * 1024
+        ),
+    )(
+        query_part,
+        memory_part,
+        output_weight,
+        first_scale,
+        own_scale,
+        out_inverse,
+        out_ratio,
+        out_scale,
+        jnp.asarray(paired_signs(width), jnp.bfloat16),
+        jnp.asarray(cosine),
+        jnp.asarray(sine),
+        document_ids[:, None],
+        document_ids[None, :],
+    )
+    return halves.transpose(1, 0, 2)
+
+
 def solution(mesh):
     return jax.shard_map(
         body,

time: 394 us -> 158 us (0.40)
  the two profiles are of different devices: /device:TPU:0 before, /device:TPU:31 now
where the time goes in v1:
time: 158 us; the launch traced here: 157 us
  Pallas kernels  127 us (80%)
  local copies, waits for them, and re-layouts  21.6 us (14%)
  matrix products  4.86 us (3%)
  other arithmetic  4.28 us (3%)
    pallas_call x1, Pallas kernels, body(): pl.pallas_call(functools.partial(fused_kernel, count), out_shape=jax.Shap...  127 us
    dynamic_slice x2, local copies, waits for them, and re-layouts, body(): lax.dynamic_index_in_dim(key_value_projection_weight, core, 1, keepdims=F...  10.4 us
    unnamed x16, local copies, waits for them, and re-layouts  5.42 us
    dot_general x1, matrix products, body(): jnp.einsum('sd,dne->nse', tokens, memory_weight, preferred_element_type=j...  3.62 us

profile of v1, /device:TPU:31, one launch (start us, length us, event | category | flops | bytes accessed | tf_op | source)
XLA Modules:
  0.0 157.5 jit_solution(7715335299771279351)
XLA Ops:
  0.0 0.0 copy-start
  0.0 0.8 fusion.18
  0.8 0.7 pad_add_fusion
  1.5 0.2 exponential_reduce_fusion
  1.6 0.7 broadcast_in_dim.32.own_scale
  2.3 0.8 exponential_bitcast_fusion
  3.1 0.1 broadcast_in_dim.36
  3.1 0.1 broadcast_in_dim.35
  3.2 0.7 fusion.14
  3.9 0.1 copy.24
  4.0 0.1 broadcast_in_dim.30.first_scale
  4.0 3.7 %constant_dynamic-slice_fusion.4 = bf16[2048,1,8,128]{3,2,1,0:T(8,128)(2,1)} fusion(bf16[2048,2,8,128]{3,2,1,0:T(8,128)(2,1)} %param.15, s32[]{:T(128)S(6)} %select_n.15), kind=kLoop, calls=%fused_computation.14 | loop fusion | bytes 8388612 | tf_op jit(solution)/shard_map/jit(dynamic_index_in_dim)/dynamic_slice | solution.py:423
  7.7 6.7 %copy.22 = bf16[2048,1,8,128]{0,3,2,1:T(8,128)(2,1)} copy(bf16[2048,1,8,128]{3,2,1,0:T(8,128)(2,1)} %constant_dynamic-slice_fusion.4) | data formatting | bytes 8388608 | tf_op jit(solution)/shard_map/jit(dynamic_index_in_dim)/dynamic_slice | solution.py:423
  14.4 0.0 copy-done
  14.4 0.0 copy-start.7
  14.4 3.6 %fusion.7.memory_part = f32[8,256,128]{2,1,0:T(8,128)S(1)} fusion(bf16[2048,1,8,128]{0,3,2,1:T(8,128)(2,1)} %copy.22, bf16[256,2048]{1,0:T(8,128)(2,1)S(1)} %copy-done), kind=kOutput, calls=%fused_computation.5 | convolution fusion | flops 1073741824 | bytes 6291456 | tf_op jit(solution)/shard_map/sd,dne->nse/dot_general | solution.py:427
  18.0 0.0 copy-done.7
  18.0 0.0 copy-start.2
  18.1 1.2 fusion.4.query_part
  19.3 0.8 copy.25.document_column
  20.1 1.2 exponential_reduce_fusion.1
  21.3 1.3 exp2.62
  22.6 0.8 broadcast_in_dim.33
  23.4 0.0 copy-done.2
  23.4 0.0 copy-start.1
  23.4 2.2 %copy-done.1 = bf16[256,8192]{1,0:T(8,128)(2,1)S(1)} copy-done((bf16[256,8192]{1,0:T(8,128)(2,1)S(1)}, bf16[256,8192]{1,0:T(8,128)(2,1)}, u32[]{:S(2)}) %copy-start.1) | copy-done | bytes 4194328
  25.6 0.0 copy-start.3
  25.6 0.9 copy-done.3
  26.5 0.0 copy-start.4
  26.5 0.9 copy-done.4
  27.4 0.0 copy-start.5
  27.4 0.7 copy-done.5
  28.1 0.0 copy-start.6
  28.1 0.7 copy-done.6
  28.8 126.7 %shard_map.127 = bf16[2,256,1024]{2,1,0:T(8,128)(2,1)S(1)} custom-call(f32[8,256,128]{2,1,0:T(8,128)S(1)} %fusion.4.query_part, f32[8,256,128]{2,1,0:T(8,128)S(1)} %fusion.7.memory_part, bf16[256,8192]{1,0:T(8,128)(2,1)S(1)} %copy-done.1, f32[8,2,128]{2,1,0:T(2,128)S(1)} %broadcast_in_dim.30.first_scale, f32[3,128]{1,0:T(4,128)S(1)} %copy-done.5, ...), custom_call_target="tpu_custom_call" | custom-call | tf_op jit(solution)/shard_map/pallas_call | solution.py:451
  155.4 2.0 %copy.26 = bf16[256,2,1024]{2,1,0:T(2,128)(2,1)} copy(bf16[256,2,1024]{2,0,1:T(8,128)(2,1)S(1)} %bitcast.28) | data formatting | bytes 2097152 | tf_op jit(solution)/shard_map/transpose | solution.py:491
Async XLA Ops:
  0.0 14.4 %copy-start = (bf16[256,2048]{1,0:T(8,128)(2,1)S(1)}, bf16[256,2048]{1,0:T(8,128)(2,1)}, u32[]{:S(2)}) copy-start(bf16[256,2048]{1,0:T(8,128)(2,1)} %param.13) | copy-start | bytes 3145732
  14.4 3.6 %copy-start.7 = (bf16[2048,8,1,128]{3,1,2,0:T(8,128)(2,1)S(1)}, bf16[2048,8,1,128]{3,1,2,0:T(8,128)(2,1)}, u32[]{:S(2)}) copy-start(bf16[2048,8,1,128]{3,1,2,0:T(8,128)(2,1)} %param.14) | copy-start | bytes 12582916
  18.0 5.3 %copy-start.2 = (f32[2,256,128]{2,1,0:T(8,128)S(1)}, f32[2,256,128]{2,1,0:T(8,128)}, u32[]{:S(2)}) copy-start(f32[2,256,128]{2,1,0:T(8,128)} %constant.44.clone.cosine_ref) | copy-start | bytes 786436
  23.4 2.2 %copy-start.1 = (bf16[256,8192]{1,0:T(8,128)(2,1)S(1)}, bf16[256,8192]{1,0:T(8,128)(2,1)}, u32[]{:S(2)}) copy-start(bf16[256,8192]{1,0:T(8,128)(2,1)} %out_weight_hbm.1) | copy-start | bytes 12582916
  25.6 0.9 copy-start.3
  26.5 0.9 copy-start.4
  27.4 0.7 copy-start.5
  28.1 0.7 copy-start.6

commit v2 on v1

--- a/solution.py
+++ b/solution.py
@@ -179,10 +179,19 @@
     angles = np.arange(length)[:, None] * frequency.astype(np.float32).astype(np.float64)[None, :]
     cosine = np.concatenate([np.cos(angles), np.cos(angles)], axis=1)
     sine = np.concatenate([-np.sin(angles), np.sin(angles)], axis=1)
-    return (
-        np.stack([cosine, np.ones_like(cosine)]).astype(np.float32),
-        np.stack([sine, np.zeros_like(sine)]).astype(np.float32),
-    )
+    return cosine.astype(np.float32), sine.astype(np.float32)
+
+
+def power(exponent, width):
+    row = jnp.full((1, width), exponent, jnp.int32)
+    size = jnp.abs(row)
+    upward = jnp.ones((1, width), jnp.float32)
+    downward = jnp.ones((1, width), jnp.float32)
+    for place in (1, 2, 4, 8, 16):
+        taken = (size & place) != 0
+        upward = jnp.where(taken, upward * 2.0**place, upward)
+        downward = jnp.where(taken, downward * 2.0**-place, downward)
+    return jnp.where(row >= 0, upward, downward)
 
 
 def turn(values, sign_matrix, norm):
@@ -202,77 +211,87 @@
     query_part,
     memory_part,
     out_weight_hbm,
-    first_scale,
-    own_scale,
-    out_inverse,
-    out_ratio,
-    out_scale,
+    document_row,
+    query_exponent,
+    partial_exponent,
+    summed_exponent,
+    out_exponent,
+    relevel,
     sign_ref,
     cosine_ref,
     sine_ref,
-    document_column,
-    document_row,
     out_ref,
     out_weight,
-    first_send,
-    first_recv,
+    first_near_send,
+    first_near_recv,
+    first_far_send,
+    first_far_recv,
     memory_pair,
     mixed,
-    second_send,
-    second_recv,
+    second_near_send,
+    second_near_recv,
+    second_far_send,
+    second_far_recv,
     total,
     weight_sem,
-    first_send_sem,
-    first_recv_sem,
-    second_send_sem,
-    second_recv_sem,
+    near_send_sem,
+    near_recv_sem,
+    far_send_sem,
+    far_recv_sem,
     pair_send_sem,
     pair_recv_sem,
 ):
     me = lax.axis_index("gx")
     core = lax.axis_index("gy")
     mate = 1 - core
+    columns_of = count // 2
+    column, row = me // 2, lax.rem(me, 2)
+    neighbour = column * 2 + 1 - row
     length, width = query_part.shape[1], query_part.shape[2]
-    span = out_inverse.shape[2]
+    span = out_ref.shape[2]
+    blocks = span // width
     norm = 1.0 / math.sqrt(width)
     chunk = 2 * width
+    mesh_ids = pl.DeviceIdType.MESH
 
     load = pltpu.make_async_copy(out_weight_hbm, out_weight, weight_sem)
     load.start()
 
+    def column_at(step):
+        return lax.rem(column + 1 + step, columns_of)
+
     barrier = pltpu.get_barrier_semaphore()
-    for away in range(1, count):
+    pl.semaphore_signal(barrier, inc=1, device_id={"gy": mate}, device_id_type=mesh_ids)
+    pl.semaphore_signal(barrier, inc=1, device_id={"gx": neighbour}, device_id_type=mesh_ids)
+    for step in range(columns_of - 1):
         pl.semaphore_signal(
             barrier,
             inc=1,
-            device_id={"gx": lax.rem(me + away, count)},
-            device_id_type=pl.DeviceIdType.MESH,
-        )
-    pl.semaphore_signal(
-        barrier, inc=1, device_id={"gy": mate}, device_id_type=pl.DeviceIdType.MESH
-    )
-    pl.semaphore_wait(barrier, count)
+            device_id={"gx": column_at(step) * 2 + row},
+            device_id_type=mesh_ids,
+        )
+    pl.semaphore_wait(barrier, columns_of + 1)
 
     small_signs = sign_ref[:width, :width]
 
-    def first_copy(away):
+    def near_copy(send, recv, stage, step):
         return pltpu.make_async_remote_copy(
-            src_ref=first_send.at[away],
-            dst_ref=first_recv.at[away],
-            send_sem=first_send_sem.at[away],
-            recv_sem=first_recv_sem.at[away],
-            device_id={"gx": lax.rem(me + away, count)},
-            device_id_type=pl.DeviceIdType.MESH,
-        )
-
-    def second_copy(away):
+            src_ref=send.at[step],
+            dst_ref=recv.at[step],
+            send_sem=near_send_sem.at[stage, step],
+            recv_sem=near_recv_sem.at[stage, step],
+            device_id={"gx": neighbour},
+            device_id_type=mesh_ids,
+        )
+
+    def far_copy(send, recv, stage, step):
         return pltpu.make_async_remote_copy(
-            src_ref=second_send.at[away],
-            dst_ref=second_recv.at[away],
-            send_sem=second_send_sem.at[away],
-            recv_sem=second_recv_sem.at[away],
-            device_id={"gx": lax.rem(me + away, count)},
-            device_id_type=pl.DeviceIdType.MESH,
+            src_ref=send.at[step],
+            dst_ref=recv.at[step],
+            send_sem=far_send_sem.at[stage, step],
+            recv_sem=far_recv_sem.at[stage, step],
+            device_id={"gx": column_at(step) * 2 + row},
+            device_id_type=mesh_ids,
         )
 
     def pair_copy(ref, place):
@@ -282,52 +301,71 @@
             send_sem=pair_send_sem.at[place],
             recv_sem=pair_recv_sem.at[place],
             device_id={"gy": mate},
-            device_id_type=pl.DeviceIdType.MESH,
-        )
-
-    def first_term(target):
-        query = saturate(turn(query_part[target], small_signs, norm) * first_scale[target, 0:1, :])
-        memory = saturate(
-            turn(memory_part[target], small_signs, norm) * first_scale[target, 1:2, :]
-        )
-        return query, memory
-
-    def first_step(away, carry):
-        query, memory = first_term(lax.rem(me + away, count))
-        first_send[away, 0] = query.astype(jnp.bfloat16)
-        first_send[away, 1] = memory.astype(jnp.bfloat16)
-        first_copy(away).start()
-        return carry
-
-    lax.fori_loop(1, count, first_step, 0)
-    query, memory = first_term(me)
+            device_id_type=mesh_ids,
+        )
+
+    def query_term(target):
+        scale = power(-query_exponent[target, 0], width)
+        return saturate(turn(query_part[target], small_signs, norm) * scale)
+
+    def memory_term(target):
+        scale = power(-partial_exponent[core, target], width)
+        return saturate(turn(memory_part[core, target], small_signs, norm) * scale)
+
+    def first_near(step, carry):
+        target = column_at(step) * 2 + 1 - row
+        first_near_send[step, 0] = query_term(target).astype(jnp.bfloat16)
+        first_near_send[step, 1] = memory_term(target).astype(jnp.bfloat16)
+        near_copy(first_near_send, first_near_recv, 0, step).start()
+        return carry
+
+    lax.fori_loop(0, columns_of, first_near, 0)
+
+    def first_joined(step):
+        target = column_at(step) * 2 + row
+        query, memory = query_term(target), memory_term(target)
+        near_copy(first_near_send, first_near_recv, 0, step).wait_recv()
+        query = query + first_near_recv[step, 0].astype(jnp.float32)
+        return query, memory + first_near_recv[step, 1].astype(jnp.float32)
+
+    def first_far(step, carry):
+        query, memory = first_joined(step)
+        first_far_send[step, 0] = query.astype(jnp.bfloat16)
+        first_far_send[step, 1] = memory.astype(jnp.bfloat16)
+        far_copy(first_far_send, first_far_recv, 0, step).start()
+        return carry
+
+    lax.fori_loop(0, columns_of - 1, first_far, 0)
+    query, memory = first_joined(columns_of - 1)
     total[:, :width] = query
     total[:, width : 2 * width] = memory
 
-    def first_sum(away, carry):
-        first_copy(away).wait_recv()
-        total[:, :width] += first_recv[away, 0].astype(jnp.float32)
-        total[:, width : 2 * width] += first_recv[away, 1].astype(jnp.float32)
-        return carry
-
-    lax.fori_loop(1, count, first_sum, 0)
-
-    level = saturate(total[:, width : 2 * width] * own_scale[1:2, :])
-    memory = turn(level * own_scale[2:3, :], small_signs, norm)
-    memory = memory * cosine_ref[core] + pltpu.roll(memory, width // 2, 1) * sine_ref[core]
-    memory_pair[core] = memory.astype(jnp.bfloat16)
+    def first_sum(step, carry):
+        far_copy(first_far_send, first_far_recv, 0, step).wait_recv()
+        total[:, :width] += first_far_recv[step, 0].astype(jnp.float32)
+        total[:, width : 2 * width] += first_far_recv[step, 1].astype(jnp.float32)
+        return carry
+
+    lax.fori_loop(0, columns_of - 1, first_sum, 0)
+
+    level_ratio = power(partial_exponent[core, me] - summed_exponent[core, me], width)
+    level = saturate(total[:, width : 2 * width] * level_ratio)
+    memory = turn(level * power(summed_exponent[core, me], width), small_signs, norm)
+    turned = memory * cosine_ref[...] + pltpu.roll(memory, width // 2, 1) * sine_ref[...]
+    memory_pair[core] = jnp.where(core == 0, turned, memory).astype(jnp.bfloat16)
     pair_copy(memory_pair, 0).start()
-    query = turn(total[:, :width] * own_scale[0:1, :], small_signs, norm)
-    query = query * cosine_ref[0] + pltpu.roll(query, width // 2, 1) * sine_ref[0]
+    query = turn(total[:, :width] * power(query_exponent[me, 0], width), small_signs, norm)
+    query = query * cosine_ref[...] + pltpu.roll(query, width // 2, 1) * sine_ref[...]
     query = query.astype(jnp.bfloat16)
+    rows = lax.broadcasted_iota(jnp.int32, (length, length), 0)
+    columns = lax.broadcasted_iota(jnp.int32, (length, length), 1)
+    documents = jnp.broadcast_to(document_row[...], (length, length)).astype(jnp.float32)
+    allowed = (rows >= columns) & (documents.T == documents)
     pair_copy(memory_pair, 0).wait_recv()
 
     scores = lax.dot_general(
         query, memory_pair[0], (((1,), (1,)), ((), ())), preferred_element_type=jnp.float32
     ) * (1.0 / math.sqrt(width))
-    rows = lax.broadcasted_iota(jnp.int32, (length, length), 0)
-    columns = lax.broadcasted_iota(jnp.int32, (length, length), 1)
-    allowed = (rows >= columns) & (document_column[...] == document_row[...])
     scores = jnp.where(allowed, scores, -jnp.inf)
     exponentials = jnp.exp(scores - jnp.max(scores, axis=-1, keepdims=True))
     weights = exponentials / jnp.sum(exponentials, axis=-1, keepdims=True)
@@ -338,50 +376,74 @@
     load.wait()
     pair_copy(mixed, 1).wait_recv()
 
+    def row_of(exponents):
+        return jnp.concatenate([power(exponent, width) for exponent in exponents], axis=1)
+
     def second_term(target, part):
         start = pl.multiple_of(target * span + part * chunk, chunk)
         both = jnp.concatenate([mixed[0], mixed[1]], axis=1)
         product = jnp.dot(
             both, out_weight[:, pl.ds(start, chunk)], preferred_element_type=jnp.float32
         )
-        scale = out_inverse[target, :, part * chunk : (part + 1) * chunk]
+        block = target * blocks + part * 2
+        scale = row_of([-out_exponent[0, block], -out_exponent[0, block + 1]])
         return saturate(turn(product, sign_ref[...], norm) * scale)
 
-    def second_step(away, carry):
-        target = lax.rem(me + away, count)
-        for part in range(span // chunk):
-            second_send[away, :, part * chunk : (part + 1) * chunk] = second_term(
-                target, part
-            ).astype(jnp.bfloat16)
-        second_copy(away).start()
-        return carry
-
-    lax.fori_loop(1, count, second_step, 0)
-    for part in range(span // chunk):
-        total[:, part * chunk : (part + 1) * chunk] = second_term(me, part)
-
-    def second_sum(away, carry):
-        second_copy(away).wait_recv()
-        for part in range(span // chunk):
-            place = slice(part * chunk, (part + 1) * chunk)
-            total[:, place] += second_recv[away, :, place].astype(jnp.float32)
-        return carry
-
-    lax.fori_loop(1, count, second_sum, 0)
-    for part in range(span // chunk):
-        place = slice(part * chunk, (part + 1) * chunk)
-        level = saturate(total[:, place] * out_ratio[:, place])
-        out_ref[core, :, place] = turn(level * out_scale[:, place], sign_ref[...], norm).astype(
-            jnp.bfloat16
-        )
+    places = [slice(part * chunk, (part + 1) * chunk) for part in range(span // chunk)]
+
+    def second_near(step, carry):
+        target = column_at(step) * 2 + 1 - row
+        for part, place in enumerate(places):
+            second_near_send[step, :, place] = second_term(target, part).astype(jnp.bfloat16)
+        near_copy(second_near_send, second_near_recv, 1, step).start()
+        return carry
+
+    lax.fori_loop(0, columns_of, second_near, 0)
+
+    def second_far(step, carry):
+        near_copy(second_near_send, second_near_recv, 1, step).wait_recv()
+        for part, place in enumerate(places):
+            joined = second_term(column_at(step) * 2 + row, part)
+            joined = joined + second_near_recv[step, :, place].astype(jnp.float32)
+            second_far_send[step, :, place] = joined.astype(jnp.bfloat16)
+        far_copy(second_far_send, second_far_recv, 1, step).start()
+        return carry
+
+    lax.fori_loop(0, columns_of - 1, second_far, 0)
+    last = columns_of - 1
+    for part, place in enumerate(places):
+        total[:, place] = second_term(me, part)
+    near_copy(second_near_send, second_near_recv, 1, last).wait_recv()
+    for place in places:
+        total[:, place] += second_near_recv[last, :, place].astype(jnp.float32)
+
+    def second_sum(step, carry):
+        far_copy(second_far_send, second_far_recv, 1, step).wait_recv()
+        for place in places:
+            total[:, place] += second_far_recv[step, :, place].astype(jnp.float32)
+        return carry
+
+    lax.fori_loop(0, columns_of - 1, second_sum, 0)
+    for part, place in enumerate(places):
+        summed = [out_exponent[0, me * blocks + part * 2 + i] for i in range(2)]
+        ending = [relevel[core, part * 2 + i] for i in range(2)]
+        ratio = row_of([start - end for start, end in zip(summed, ending)])
+        level = saturate(total[:, place] * ratio) * row_of(ending)
+        out_ref[core, :, place] = turn(level, sign_ref[...], norm).astype(jnp.bfloat16)
     pair_copy(out_ref, 2).start()
 
-    def drain(away, carry):
-        first_copy(away).wait_send()
-        second_copy(away).wait_send()
-        return carry
-
-    lax.fori_loop(1, count, drain, 0)
+    def drain_near(step, carry):
+        near_copy(first_near_send, first_near_recv, 0, step).wait_send()
+        near_copy(second_near_send, second_near_recv, 1, step).wait_send()
+        return carry
+
+    def drain_far(step, carry):
+        far_copy(first_far_send, first_far_recv, 0, step).wait_send()
+        far_copy(second_far_send, second_far_recv, 1, step).wait_send()
+        return carry
+
+    lax.fori_loop(0, columns_of, drain_near, 0)
+    lax.fori_loop(0, columns_of - 1, drain_far, 0)
     pair_copy(memory_pair, 0).wait_send()
     pair_copy(mixed, 1).wait_send()
     pair_copy(out_ref, 2).wait()
@@ -405,7 +467,8 @@
     heads = query_weight.shape[1]
     memory_heads = key_value_projection_weight.shape[2]
     span = output_weight.shape[1] // count
-    if not (count == heads == memory_heads and lax.axis_size("gy") == 2 and span % (2 * width) == 0):
+    even = count % 2 == 0 and lax.axis_size("gy") == 2 and span % (2 * width) == 0
+    if not (even and count == heads == memory_heads):
         return plain_body(
             tokens,
             query_weight,
@@ -418,55 +481,40 @@
             output_exponent,
             output_relevel,
         )
-    me = lax.axis_index("gx")
-    core = lax.axis_index("gy")
-    memory_weight = lax.dynamic_index_in_dim(key_value_projection_weight, core, 1, keepdims=False)
     query_part = jnp.einsum(
         "sd,dpe->pse", tokens, query_weight[:, :, 0, :], preferred_element_type=jnp.float32
     )
-    memory_part = jnp.einsum("sd,dne->nse", tokens, memory_weight, preferred_element_type=jnp.float32)
-
-    def power(exponent):
-        return jnp.exp2(exponent.astype(jnp.float32))
-
-    partial_exponent = lax.dynamic_index_in_dim(key_value_partial_exponents, core, 0, keepdims=False)
-    summed_exponent = lax.dynamic_index_in_dim(key_value_summed_exponents, core, 0, keepdims=False)
-    first_scale = jnp.broadcast_to(
-        power(-jnp.stack([query_exponent[:, 0], partial_exponent], axis=1))[:, :, None],
-        (count, 2, width),
-    )
-    own = jnp.stack(
-        [query_exponent[:, 0], partial_exponent - summed_exponent, summed_exponent], axis=0
-    )
-    own = lax.dynamic_index_in_dim(own, me, 1, keepdims=True)
-    own_scale = jnp.broadcast_to(power(own), (3, width))
-    blocks = span // width
-    out_inverse = jnp.repeat(power(-output_exponent[0]), width).reshape(count, 1, span)
-    relevel = lax.dynamic_index_in_dim(output_relevel, core, 0, keepdims=False)
-    here = lax.dynamic_slice_in_dim(output_exponent[0], me * blocks, blocks, 0)
-    out_ratio = jnp.repeat(power(here - relevel), width)[None]
-    out_scale = jnp.repeat(power(relevel), width)[None]
+    memory_part = jnp.einsum(
+        "sd,dcne->cnse", tokens, key_value_projection_weight, preferred_element_type=jnp.float32
+    )
     cosine, sine = rotary_tables(length, width)
     vmem = pl.BlockSpec(memory_space=pltpu.VMEM)
+    smem = pl.BlockSpec(memory_space=pltpu.SMEM)
+    half = count // 2
+    bf16 = jnp.bfloat16
     halves = pl.pallas_call(
         functools.partial(fused_kernel, count),
-        out_shape=jax.ShapeDtypeStruct((2, length, span), jnp.bfloat16),
-        in_specs=[vmem, vmem, pl.BlockSpec(memory_space=pl.ANY)] + [vmem] * 10,
+        out_shape=jax.ShapeDtypeStruct((2, length, span), bf16),
+        in_specs=[vmem, vmem, pl.BlockSpec(memory_space=pl.ANY), vmem] + [smem] * 5 + [vmem] * 3,
         out_specs=vmem,
         scratch_shapes=[
-            pltpu.VMEM(output_weight.shape, jnp.bfloat16),
-            pltpu.VMEM((count, 2, length, width), jnp.bfloat16),
-            pltpu.VMEM((count, 2, length, width), jnp.bfloat16),
-            pltpu.VMEM((2, length, width), jnp.bfloat16),
-            pltpu.VMEM((2, length, width), jnp.bfloat16),
-            pltpu.VMEM((count, length, span), jnp.bfloat16),
-            pltpu.VMEM((count, length, span), jnp.bfloat16),
+            pltpu.VMEM(output_weight.shape, bf16),
+            pltpu.VMEM((half, 2, length, width), bf16),
+            pltpu.VMEM((half, 2, length, width), bf16),
+            pltpu.VMEM((half - 1, 2, length, width), bf16),
+            pltpu.VMEM((half - 1, 2, length, width), bf16),
+            pltpu.VMEM((2, length, width), bf16),
+            pltpu.VMEM((2, length, width), bf16),
+            pltpu.VMEM((half, length, span), bf16),
+            pltpu.VMEM((half, length, span), bf16),
+            pltpu.VMEM((half - 1, length, span), bf16),
+            pltpu.VMEM((half - 1, length, span), bf16),
             pltpu.VMEM((length, span), jnp.float32),
             pltpu.SemaphoreType.DMA,
-            pltpu.SemaphoreType.DMA((count,)),
-            pltpu.SemaphoreType.DMA((count,)),
-            pltpu.SemaphoreType.DMA((count,)),
-            pltpu.SemaphoreType.DMA((count,)),
+            pltpu.SemaphoreType.DMA((2, half)),
+            pltpu.SemaphoreType.DMA((2, half)),
+            pltpu.SemaphoreType.DMA((2, half - 1)),
+            pltpu.SemaphoreType.DMA((2, half - 1)),
             pltpu.SemaphoreType.DMA((3,)),
             pltpu.SemaphoreType.DMA((3,)),
         ],
@@ -477,16 +525,15 @@
         query_part,
         memory_part,
         output_weight,
-        first_scale,
-        own_scale,
-        out_inverse,
-        out_ratio,
-        out_scale,
-        jnp.asarray(paired_signs(width), jnp.bfloat16),
+        document_ids[None, :],
+        query_exponent,
+        key_value_partial_exponents,
+        key_value_summed_exponents,
+        output_exponent,
+        output_relevel,
+        jnp.asarray(paired_signs(width), bf16),
         jnp.asarray(cosine),
         jnp.asarray(sine),
-        document_ids[:, None],
-        document_ids[None, :],
     )
     return halves.transpose(1, 0, 2)
 

time: 158 us -> 99 us (0.63)
  the two profiles are of different devices: /device:TPU:31 before, /device:TPU:0 now
where the time goes in v2:
time: 99 us; the launch traced here: 98.8 us
  Pallas kernels  88.3 us (89%)
  matrix products  5.96 us (6%)
  local copies, waits for them, and re-layouts  4.39 us (4%)
    pallas_call x1, Pallas kernels, body(): pl.pallas_call(functools.partial(fused_kernel, count), out_shape=jax.Shap...  88.3 us
    dot_general x1, matrix products, body(): jnp.einsum('sd,dpe->pse', tokens, query_weight[:, :, 0, :], preferred_ele...  3.58 us
    dot_general x1, matrix products, body(): jnp.einsum('sd,dcne->cnse', tokens, key_value_projection_weight, preferre...  2.38 us
    unnamed x23, local copies, waits for them, and re-layouts  2.34 us
    transpose x1, local copies, waits for them, and re-layouts, body(): return halves.transpose(1, 0, 2)  2.05 us

profile of v2, /device:TPU:0, one launch (start us, length us, event | category | flops | bytes accessed | tf_op | source)
XLA Modules:
  0.0 98.8 jit_solution(10019915355495501176)
XLA Ops:
  0.0 0.0 copy-start
  0.0 0.8 copy.18.query_exponent
  0.8 0.4 copy-done
  1.2 0.0 copy-start.10
  1.2 3.6 %fusion.7.query_part = f32[8,256,128]{2,1,0:T(8,128)S(1)} fusion(bf16[2048,8,128]{2,1,0:T(8,128)(2,1)} %bitcast.17, bf16[256,2048]{1,0:T(8,128)(2,1)S(1)} %copy-done), kind=kOutput, calls=%fused_computation.5 | convolution fusion | flops 1073741824 | bytes 6291456 | tf_op jit(solution)/shard_map/sd,dpe->pse/dot_general | solution.py:484
  4.8 1.1 %copy-done.10 = bf16[2048,2,8,128]{3,2,1,0:T(8,128)(2,1)S(1)} copy-done((bf16[2048,2,8,128]{3,2,1,0:T(8,128)(2,1)S(1)}, bf16[2048,2,8,128]{3,2,1,0:T(8,128)(2,1)}, u32[]{:S(2)}) %copy-start.10) | copy-done | bytes 8388632
  5.9 0.0 copy-start.1
  5.9 0.0 copy-start.2
  5.9 0.0 copy-start.3
  5.9 0.0 copy-start.4
  5.9 0.0 copy-start.5
  5.9 0.0 copy-start.6
  5.9 0.0 copy-start.7
  5.9 0.0 copy-start.8
  5.9 0.0 copy-start.9
  6.0 2.4 %fusion.4.memory_part = f32[2,8,256,128]{3,2,1,0:T(8,128)S(1)} fusion(bf16[2048,2,8,128]{3,2,1,0:T(8,128)(2,1)S(1)} %copy-done.10, bf16[256,2048]{1,0:T(8,128)(2,1)S(1)} %copy-done), kind=kOutput, calls=%fused_computation.4 | convolution fusion | flops 2147483648 | bytes 11534336 | tf_op jit(solution)/shard_map/sd,dcne->cnse/dot_general | solution.py:487
  8.3 0.0 copy-done.1
  8.4 0.0 copy-done.2
  8.4 0.0 copy-done.3
  8.4 0.0 copy-done.4
  8.4 0.0 copy-done.5
  8.4 0.0 copy-done.6
  8.4 0.0 copy-done.7
  8.4 0.0 copy-done.8
  8.4 0.0 copy-done.9
  8.4 88.3 %shard_map.127 = bf16[2,256,1024]{2,1,0:T(8,128)(2,1)S(1)} custom-call(f32[8,256,128]{2,1,0:T(8,128)S(1)} %fusion.7.query_part, f32[2,8,256,128]{3,2,1,0:T(8,128)S(1)} %fusion.4.memory_part, bf16[256,8192]{1,0:T(8,128)(2,1)S(1)} %copy-done.1, s32[1,256]{1,0:T(1,128)S(1)} %bitcast.16, s32[8,1]{1,0:T(8,128)S(1)} %copy.18.query_exponent, s32[2,8]{1,0:T(2,128)S(1)} %copy-done.6, ...), custom_call_target="tpu_custom_call" | custom-call | tf_op jit(solution)/shard_map/pallas_call | solution.py:495
  96.7 2.0 %copy.19 = bf16[256,2,1024]{2,1,0:T(2,128)(2,1)} copy(bf16[256,2,1024]{2,0,1:T(8,128)(2,1)S(1)} %bitcast.15) | data formatting | bytes 2097152 | tf_op jit(solution)/shard_map/transpose | solution.py:538
Async XLA Ops:
  0.0 1.2 %copy-start = (bf16[256,2048]{1,0:T(8,128)(2,1)S(1)}, bf16[256,2048]{1,0:T(8,128)(2,1)}, u32[]{:S(2)}) copy-start(bf16[256,2048]{1,0:T(8,128)(2,1)} %param.13) | copy-start | bytes 3145732
  1.2 4.6 %copy-start.10 = (bf16[2048,2,8,128]{3,2,1,0:T(8,128)(2,1)S(1)}, bf16[2048,2,8,128]{3,2,1,0:T(8,128)(2,1)}, u32[]{:S(2)}) copy-start(bf16[2048,2,8,128]{3,2,1,0:T(8,128)(2,1)} %param.15) | copy-start | bytes 25165828
  5.9 2.5 %copy-start.1 = (bf16[256,8192]{1,0:T(8,128)(2,1)S(1)}, bf16[256,8192]{1,0:T(8,128)(2,1)}, u32[]{:S(2)}) copy-start(bf16[256,8192]{1,0:T(8,128)(2,1)} %out_weight_hbm.1) | copy-start | bytes 12582916
  5.9 2.5 %copy-start.2 = (f32[256,128]{1,0:T(8,128)S(1)}, f32[256,128]{1,0:T(8,128)}, u32[]{:S(2)}) copy-start(f32[256,128]{1,0:T(8,128)} %constant.8.clone.sine_ref) | copy-start | bytes 393220
  5.9 2.5 %copy-start.3 = (f32[256,128]{1,0:T(8,128)S(1)}, f32[256,128]{1,0:T(8,128)}, u32[]{:S(2)}) copy-start(f32[256,128]{1,0:T(8,128)} %constant.7.clone.cosine_ref) | copy-start | bytes 393220
  5.9 2.5 %copy-start.4 = (bf16[256,256]{1,0:T(8,128)(2,1)S(1)}, bf16[256,256]{1,0:T(8,128)(2,1)}, u32[]{:S(2)}) copy-start(bf16[256,256]{1,0:T(8,128)(2,1)} %constant.6.clone.sign_ref) | copy-start | bytes 393220
  5.9 2.5 %copy-start.5 = (s32[256]{0:T(256)S(1)}, s32[256]{0:T(256)}, u32[]{:S(2)}) copy-start(s32[256]{0:T(256)} %param.17) | copy-start | bytes 3076
  5.9 2.5 %copy-start.6 = (s32[2,8]{1,0:T(2,128)S(1)}, s32[2,8]{1,0:T(2,128)}, u32[]{:S(2)}) copy-start(s32[2,8]{1,0:T(2,128)} %partial_exponent.1) | copy-start | bytes 196
  5.9 2.5 %copy-start.7 = (s32[2,8]{1,0:T(2,128)S(1)}, s32[2,8]{1,0:T(2,128)}, u32[]{:S(2)}) copy-start(s32[2,8]{1,0:T(2,128)} %summed_exponent.1) | copy-start | bytes 196
  5.9 2.5 %copy-start.8 = (s32[2,8]{1,0:T(2,128)S(1)}, s32[2,8]{1,0:T(2,128)}, u32[]{:S(2)}) copy-start(s32[2,8]{1,0:T(2,128)} %relevel.1) | copy-start | bytes 196
  5.9 2.5 %copy-start.9 = (s32[1,64]{1,0:T(1,128)S(1)}, s32[1,64]{1,0:T(1,128)}, u32[]{:S(2)}) copy-start(s32[1,64]{1,0:T(1,128)} %out_exponent.1) | copy-start | bytes 772

commit v3 on v2

--- a/solution.py
+++ b/solution.py
@@ -232,7 +232,9 @@
     second_near_recv,
     second_far_send,
     second_far_recv,
+    first_total,
     total,
+    bias,
     weight_sem,
     near_send_sem,
     near_recv_sem,
@@ -240,6 +242,12 @@
     far_recv_sem,
     pair_send_sem,
     pair_recv_sem,
+    piece_near_send,
+    piece_near_recv,
+    piece_far_send,
+    piece_far_recv,
+    out_send_sem,
+    out_recv_sem,
 ):
     me = lax.axis_index("gx")
     core = lax.axis_index("gy")
@@ -337,36 +345,38 @@
 
     lax.fori_loop(0, columns_of - 1, first_far, 0)
     query, memory = first_joined(columns_of - 1)
-    total[:, :width] = query
-    total[:, width : 2 * width] = memory
+    first_total[0] = query
+    first_total[1] = memory
+
+    rows = lax.broadcasted_iota(jnp.int32, (length, length), 0)
+    columns = lax.broadcasted_iota(jnp.int32, (length, length), 1)
+    documents = jnp.broadcast_to(document_row[...], (length, length)).astype(jnp.float32)
+    allowed = (rows >= columns) & (documents.T == documents)
+    bias[...] = jnp.where(allowed, 0.0, -jnp.inf)
 
     def first_sum(step, carry):
         far_copy(first_far_send, first_far_recv, 0, step).wait_recv()
-        total[:, :width] += first_far_recv[step, 0].astype(jnp.float32)
-        total[:, width : 2 * width] += first_far_recv[step, 1].astype(jnp.float32)
+        first_total[0] += first_far_recv[step, 0].astype(jnp.float32)
+        first_total[1] += first_far_recv[step, 1].astype(jnp.float32)
         return carry
 
     lax.fori_loop(0, columns_of - 1, first_sum, 0)
 
     level_ratio = power(partial_exponent[core, me] - summed_exponent[core, me], width)
-    level = saturate(total[:, width : 2 * width] * level_ratio)
+    level = saturate(first_total[1] * level_ratio)
     memory = turn(level * power(summed_exponent[core, me], width), small_signs, norm)
     turned = memory * cosine_ref[...] + pltpu.roll(memory, width // 2, 1) * sine_ref[...]
     memory_pair[core] = jnp.where(core == 0, turned, memory).astype(jnp.bfloat16)
     pair_copy(memory_pair, 0).start()
-    query = turn(total[:, :width] * power(query_exponent[me, 0], width), small_signs, norm)
+    query = turn(first_total[0] * power(query_exponent[me, 0], width), small_signs, norm)
     query = query * cosine_ref[...] + pltpu.roll(query, width // 2, 1) * sine_ref[...]
     query = query.astype(jnp.bfloat16)
-    rows = lax.broadcasted_iota(jnp.int32, (length, length), 0)
-    columns = lax.broadcasted_iota(jnp.int32, (length, length), 1)
-    documents = jnp.broadcast_to(document_row[...], (length, length)).astype(jnp.float32)
-    allowed = (rows >= columns) & (documents.T == documents)
     pair_copy(memory_pair, 0).wait_recv()
 
     scores = lax.dot_general(
         query, memory_pair[0], (((1,), (1,)), ((), ())), preferred_element_type=jnp.float32
     ) * (1.0 / math.sqrt(width))
-    scores = jnp.where(allowed, scores, -jnp.inf)
+    scores = scores + bias[...]
     exponentials = jnp.exp(scores - jnp.max(scores, axis=-1, keepdims=True))
     weights = exponentials / jnp.sum(exponentials, axis=-1, keepdims=True)
     mixed[core] = jnp.dot(
@@ -380,7 +390,7 @@
         return jnp.concatenate([power(exponent, width) for exponent in exponents], axis=1)
 
     def second_term(target, part):
-        start = pl.multiple_of(target * span + part * chunk, chunk)
+        start = pl.multiple_of((target * (span // chunk) + part) * chunk, chunk)
         both = jnp.concatenate([mixed[0], mixed[1]], axis=1)
         product = jnp.dot(
             both, out_weight[:, pl.ds(start, chunk)], preferred_element_type=jnp.float32
@@ -389,64 +399,108 @@
         scale = row_of([-out_exponent[0, block], -out_exponent[0, block + 1]])
         return saturate(turn(product, sign_ref[...], norm) * scale)
 
-    places = [slice(part * chunk, (part + 1) * chunk) for part in range(span // chunk)]
-
-    def second_near(step, carry):
-        target = column_at(step) * 2 + 1 - row
-        for part, place in enumerate(places):
-            second_near_send[step, :, place] = second_term(target, part).astype(jnp.bfloat16)
-        near_copy(second_near_send, second_near_recv, 1, step).start()
-        return carry
-
-    lax.fori_loop(0, columns_of, second_near, 0)
-
-    def second_far(step, carry):
-        near_copy(second_near_send, second_near_recv, 1, step).wait_recv()
-        for part, place in enumerate(places):
-            joined = second_term(column_at(step) * 2 + row, part)
-            joined = joined + second_near_recv[step, :, place].astype(jnp.float32)
-            second_far_send[step, :, place] = joined.astype(jnp.bfloat16)
-        far_copy(second_far_send, second_far_recv, 1, step).start()
-        return carry
-
-    lax.fori_loop(0, columns_of - 1, second_far, 0)
-    last = columns_of - 1
-    for part, place in enumerate(places):
-        total[:, place] = second_term(me, part)
-    near_copy(second_near_send, second_near_recv, 1, last).wait_recv()
-    for place in places:
-        total[:, place] += second_near_recv[last, :, place].astype(jnp.float32)
-
-    def second_sum(step, carry):
-        far_copy(second_far_send, second_far_recv, 1, step).wait_recv()
-        for place in places:
-            total[:, place] += second_far_recv[step, :, place].astype(jnp.float32)
-        return carry
-
-    lax.fori_loop(0, columns_of - 1, second_sum, 0)
-    for part, place in enumerate(places):
+    parts = span // chunk
+    ahead = min(3, parts)
+    near_total, far_total = columns_of * parts, (columns_of - 1) * parts
+
+    def piece_copy(kind, piece):
+        send, recv, send_sem, recv_sem, target = {
+            "near": (second_near_send, second_near_recv, piece_near_send, piece_near_recv, None),
+            "far": (second_far_send, second_far_recv, piece_far_send, piece_far_recv, 1),
+        }[kind]
+        if target is None:
+            target = neighbour
+        else:
+            target = column_at(piece // parts) * 2 + row
+        return pltpu.make_async_remote_copy(
+            src_ref=send.at[piece],
+            dst_ref=recv.at[piece],
+            send_sem=send_sem.at[piece],
+            recv_sem=recv_sem.at[piece],
+            device_id={"gx": target},
+            device_id_type=mesh_ids,
+        )
+
+    def second_near(piece, carry):
+        target = column_at(piece // parts) * 2 + 1 - row
+        second_near_send[piece] = second_term(target, piece % parts).astype(jnp.bfloat16)
+        piece_copy("near", piece).start()
+        return carry
+
+    def second_joined(piece):
+        term = second_term(column_at(piece // parts) * 2 + row, piece % parts)
+        piece_copy("near", piece).wait_recv()
+        return term + second_near_recv[piece].astype(jnp.float32)
+
+    def second_far(piece, carry):
+        second_near(piece + ahead, 0)
+        second_far_send[piece] = second_joined(piece).astype(jnp.bfloat16)
+        piece_copy("far", piece).start()
+        return carry
+
+    lax.fori_loop(0, ahead, second_near, 0)
+    lax.fori_loop(0, far_total, second_far, 0)
+    lax.fori_loop(far_total + ahead, near_total, second_near, 0)
+
+    def second_own(part, carry):
+        total[part] = second_joined(far_total + part)
+        return carry
+
+    lax.fori_loop(0, parts, second_own, 0)
+
+    def second_sum(piece, carry):
+        piece_copy("far", piece).wait_recv()
+        total[piece % parts] += second_far_recv[piece].astype(jnp.float32)
+        return carry
+
+    lax.fori_loop(0, far_total - parts, second_sum, 0)
+
+    def out_copy(part):
+        place = slice(part * chunk, (part + 1) * chunk)
+        return pltpu.make_async_remote_copy(
+            src_ref=out_ref.at[core, :, place],
+            dst_ref=out_ref.at[core, :, place],
+            send_sem=out_send_sem.at[part],
+            recv_sem=out_recv_sem.at[part],
+            device_id={"gy": mate},
+            device_id_type=mesh_ids,
+        )
+
+    for part in range(parts):
+        second_sum(far_total - parts + part, 0)
         summed = [out_exponent[0, me * blocks + part * 2 + i] for i in range(2)]
         ending = [relevel[core, part * 2 + i] for i in range(2)]
         ratio = row_of([start - end for start, end in zip(summed, ending)])
-        level = saturate(total[:, place] * ratio) * row_of(ending)
-        out_ref[core, :, place] = turn(level, sign_ref[...], norm).astype(jnp.bfloat16)
-    pair_copy(out_ref, 2).start()
+        level = saturate(total[part] * ratio) * row_of(ending)
+        out_ref[core, :, part * chunk : (part + 1) * chunk] = turn(
+            level, sign_ref[...], norm
+        ).astype(jnp.bfloat16)
+        out_copy(part).start()
 
     def drain_near(step, carry):
         near_copy(first_near_send, first_near_recv, 0, step).wait_send()
-        near_copy(second_near_send, second_near_recv, 1, step).wait_send()
         return carry
 
     def drain_far(step, carry):
         far_copy(first_far_send, first_far_recv, 0, step).wait_send()
-        far_copy(second_far_send, second_far_recv, 1, step).wait_send()
-        return carry
-
+        return carry
+
+    def drain_near_piece(piece, carry):
+        piece_copy("near", piece).wait_send()
+        return carry
+
+    def drain_far_piece(piece, carry):
+        piece_copy("far", piece).wait_send()
+        return carry
+
+    lax.fori_loop(0, near_total, drain_near_piece, 0)
+    lax.fori_loop(0, far_total, drain_far_piece, 0)
     lax.fori_loop(0, columns_of, drain_near, 0)
     lax.fori_loop(0, columns_of - 1, drain_far, 0)
     pair_copy(memory_pair, 0).wait_send()
     pair_copy(mixed, 1).wait_send()
-    pair_copy(out_ref, 2).wait()
+    for part in range(parts):
+        out_copy(part).wait()
 
 
 def body(
@@ -491,6 +545,7 @@
     vmem = pl.BlockSpec(memory_space=pltpu.VMEM)
     smem = pl.BlockSpec(memory_space=pltpu.SMEM)
     half = count // 2
+    parts = span // (2 * width)
     bf16 = jnp.bfloat16
     halves = pl.pallas_call(
         functools.partial(fused_kernel, count),
@@ -505,18 +560,26 @@
             pltpu.VMEM((half - 1, 2, length, width), bf16),
             pltpu.VMEM((2, length, width), bf16),
             pltpu.VMEM((2, length, width), bf16),
-            pltpu.VMEM((half, length, span), bf16),
-            pltpu.VMEM((half, length, span), bf16),
-            pltpu.VMEM((half - 1, length, span), bf16),
-            pltpu.VMEM((half - 1, length, span), bf16),
-            pltpu.VMEM((length, span), jnp.float32),
+            pltpu.VMEM((half * parts, length, 2 * width), bf16),
+            pltpu.VMEM((half * parts, length, 2 * width), bf16),
+            pltpu.VMEM(((half - 1) * parts, length, 2 * width), bf16),
+            pltpu.VMEM(((half - 1) * parts, length, 2 * width), bf16),
+            pltpu.VMEM((2, length, width), jnp.float32),
+            pltpu.VMEM((parts, length, 2 * width), jnp.float32),
+            pltpu.VMEM((length, length), jnp.float32),
             pltpu.SemaphoreType.DMA,
-            pltpu.SemaphoreType.DMA((2, half)),
-            pltpu.SemaphoreType.DMA((2, half)),
-            pltpu.SemaphoreType.DMA((2, half - 1)),
-            pltpu.SemaphoreType.DMA((2, half - 1)),
-            pltpu.SemaphoreType.DMA((3,)),
-            pltpu.SemaphoreType.DMA((3,)),
+            pltpu.SemaphoreType.DMA((1, half)),
+            pltpu.SemaphoreType.DMA((1, half)),
+            pltpu.SemaphoreType.DMA((1, half - 1)),
+            pltpu.SemaphoreType.DMA((1, half - 1)),
+            pltpu.SemaphoreType.DMA((2,)),
+            pltpu.SemaphoreType.DMA((2,)),
+            pltpu.SemaphoreType.DMA((half * parts,)),
+            pltpu.SemaphoreType.DMA((half * parts,)),
+            pltpu.SemaphoreType.DMA(((half - 1) * parts,)),
+            pltpu.SemaphoreType.DMA(((half - 1) * parts,)),
+            pltpu.SemaphoreType.DMA((parts,)),
+            pltpu.SemaphoreType.DMA((parts,)),
         ],
         compiler_params=pltpu.CompilerParams(
             collective_id=0, has_side_effects=True, vmem_limit_bytes=40 * 1024 * 1024

time: 99 us -> 90.3 us (0.912)
  Pallas kernels: 88.3 us -> 79.2 us
    pallas_call x1, Pallas kernels: 88.3 us -> 79.2 us  [body(): pl.pallas_call(functools.partial(fused_kernel, count), out_shape=jax.Shap...]
where the time goes in v3:
time: 90.3 us; the launch traced here: 89.7 us
  Pallas kernels  79.2 us (88%)
  matrix products  5.96 us (7%)
  local copies, waits for them, and re-layouts  4.39 us (5%)
    pallas_call x1, Pallas kernels, body(): pl.pallas_call(functools.partial(fused_kernel, count), out_shape=jax.Shap...  79.2 us
    dot_general x1, matrix products, body(): jnp.einsum('sd,dpe->pse', tokens, query_weight[:, :, 0, :], preferred_ele...  3.58 us
    dot_general x1, matrix products, body(): jnp.einsum('sd,dcne->cnse', tokens, key_value_projection_weight, preferre...  2.38 us
    unnamed x23, local copies, waits for them, and re-layouts  2.34 us
    transpose x1, local copies, waits for them, and re-layouts, body(): return halves.transpose(1, 0, 2)  2.05 us

profile of v3, /device:TPU:0, one launch (start us, length us, event | category | flops | bytes accessed | tf_op | source)
XLA Modules:
  0.0 89.7 jit_solution(300560147315860237)
XLA Ops:
  0.0 0.0 copy-start
  0.0 0.8 copy.18.query_exponent
  0.8 0.4 copy-done
  1.2 0.0 copy-start.10
  1.2 3.6 %fusion.7.query_part = f32[8,256,128]{2,1,0:T(8,128)S(1)} fusion(bf16[2048,8,128]{2,1,0:T(8,128)(2,1)} %bitcast.17, bf16[256,2048]{1,0:T(8,128)(2,1)S(1)} %copy-done), kind=kOutput, calls=%fused_computation.5 | convolution fusion | flops 1073741824 | bytes 6291456 | tf_op jit(solution)/shard_map/sd,dpe->pse/dot_general | solution.py:538
  4.8 1.1 %copy-done.10 = bf16[2048,2,8,128]{3,2,1,0:T(8,128)(2,1)S(1)} copy-done((bf16[2048,2,8,128]{3,2,1,0:T(8,128)(2,1)S(1)}, bf16[2048,2,8,128]{3,2,1,0:T(8,128)(2,1)}, u32[]{:S(2)}) %copy-start.10) | copy-done | bytes 8388632
  5.9 0.0 copy-start.1
  5.9 0.0 copy-start.2
  5.9 0.0 copy-start.3
  5.9 0.0 copy-start.4
  5.9 0.0 copy-start.5
  5.9 0.0 copy-start.6
  5.9 0.0 copy-start.7
  5.9 0.0 copy-start.8
  5.9 0.0 copy-start.9
  6.0 2.4 %fusion.4.memory_part = f32[2,8,256,128]{3,2,1,0:T(8,128)S(1)} fusion(bf16[2048,2,8,128]{3,2,1,0:T(8,128)(2,1)S(1)} %copy-done.10, bf16[256,2048]{1,0:T(8,128)(2,1)S(1)} %copy-done), kind=kOutput, calls=%fused_computation.4 | convolution fusion | flops 2147483648 | bytes 11534336 | tf_op jit(solution)/shard_map/sd,dcne->cnse/dot_general | solution.py:541
  8.3 0.0 copy-done.1
  8.4 0.0 copy-done.2
  8.4 0.0 copy-done.3
  8.4 0.0 copy-done.4
  8.4 0.0 copy-done.5
  8.4 0.0 copy-done.6
  8.4 0.0 copy-done.7
  8.4 0.0 copy-done.8
  8.4 0.0 copy-done.9
  8.4 79.2 %shard_map.127 = bf16[2,256,1024]{2,1,0:T(8,128)(2,1)S(1)} custom-call(f32[8,256,128]{2,1,0:T(8,128)S(1)} %fusion.7.query_part, f32[2,8,256,128]{3,2,1,0:T(8,128)S(1)} %fusion.4.memory_part, bf16[256,8192]{1,0:T(8,128)(2,1)S(1)} %copy-done.1, s32[1,256]{1,0:T(1,128)S(1)} %bitcast.16, s32[8,1]{1,0:T(8,128)S(1)} %copy.18.query_exponent, s32[2,8]{1,0:T(2,128)S(1)} %copy-done.6, ...), custom_call_target="tpu_custom_call" | custom-call | tf_op jit(solution)/shard_map/pallas_call | solution.py:550
  87.6 2.0 %copy.19 = bf16[256,2,1024]{2,1,0:T(2,128)(2,1)} copy(bf16[256,2,1024]{2,0,1:T(8,128)(2,1)S(1)} %bitcast.15) | data formatting | bytes 2097152 | tf_op jit(solution)/shard_map/transpose | solution.py:601
Async XLA Ops:
  0.0 1.2 %copy-start = (bf16[256,2048]{1,0:T(8,128)(2,1)S(1)}, bf16[256,2048]{1,0:T(8,128)(2,1)}, u32[]{:S(2)}) copy-start(bf16[256,2048]{1,0:T(8,128)(2,1)} %param.13) | copy-start | bytes 3145732
  1.2 4.6 %copy-start.10 = (bf16[2048,2,8,128]{3,2,1,0:T(8,128)(2,1)S(1)}, bf16[2048,2,8,128]{3,2,1,0:T(8,128)(2,1)}, u32[]{:S(2)}) copy-start(bf16[2048,2,8,128]{3,2,1,0:T(8,128)(2,1)} %param.15) | copy-start | bytes 25165828
  5.9 2.5 %copy-start.1 = (bf16[256,8192]{1,0:T(8,128)(2,1)S(1)}, bf16[256,8192]{1,0:T(8,128)(2,1)}, u32[]{:S(2)}) copy-start(bf16[256,8192]{1,0:T(8,128)(2,1)} %out_weight_hbm.1) | copy-start | bytes 12582916
  5.9 2.5 %copy-start.2 = (f32[256,128]{1,0:T(8,128)S(1)}, f32[256,128]{1,0:T(8,128)}, u32[]{:S(2)}) copy-start(f32[256,128]{1,0:T(8,128)} %constant.8.clone.sine_ref) | copy-start | bytes 393220
  5.9 2.5 %copy-start.3 = (f32[256,128]{1,0:T(8,128)S(1)}, f32[256,128]{1,0:T(8,128)}, u32[]{:S(2)}) copy-start(f32[256,128]{1,0:T(8,128)} %constant.7.clone.cosine_ref) | copy-start | bytes 393220
  5.9 2.5 %copy-start.4 = (bf16[256,256]{1,0:T(8,128)(2,1)S(1)}, bf16[256,256]{1,0:T(8,128)(2,1)}, u32[]{:S(2)}) copy-start(bf16[256,256]{1,0:T(8,128)(2,1)} %constant.6.clone.sign_ref) | copy-start | bytes 393220
  5.9 2.5 %copy-start.5 = (s32[256]{0:T(256)S(1)}, s32[256]{0:T(256)}, u32[]{:S(2)}) copy-start(s32[256]{0:T(256)} %param.17) | copy-start | bytes 3076
  5.9 2.5 %copy-start.6 = (s32[2,8]{1,0:T(2,128)S(1)}, s32[2,8]{1,0:T(2,128)}, u32[]{:S(2)}) copy-start(s32[2,8]{1,0:T(2,128)} %partial_exponent.1) | copy-start | bytes 196
  5.9 2.5 %copy-start.7 = (s32[2,8]{1,0:T(2,128)S(1)}, s32[2,8]{1,0:T(2,128)}, u32[]{:S(2)}) copy-start(s32[2,8]{1,0:T(2,128)} %summed_exponent.1) | copy-start | bytes 196
  5.9 2.5 %copy-start.8 = (s32[2,8]{1,0:T(2,128)S(1)}, s32[2,8]{1,0:T(2,128)}, u32[]{:S(2)}) copy-start(s32[2,8]{1,0:T(2,128)} %relevel.1) | copy-start | bytes 196
  5.9 2.5 %copy-start.9 = (s32[1,64]{1,0:T(1,128)S(1)}, s32[1,64]{1,0:T(1,128)}, u32[]{:S(2)}) copy-start(s32[1,64]{1,0:T(1,128)} %out_exponent.1) | copy-start | bytes 772

commit v4 on v3

--- a/solution.py
+++ b/solution.py
@@ -282,22 +282,22 @@
 
     small_signs = sign_ref[:width, :width]
 
-    def near_copy(send, recv, stage, step):
+    def first_near_copy(kind, step):
         return pltpu.make_async_remote_copy(
-            src_ref=send.at[step],
-            dst_ref=recv.at[step],
-            send_sem=near_send_sem.at[stage, step],
-            recv_sem=near_recv_sem.at[stage, step],
+            src_ref=first_near_send.at[kind, step],
+            dst_ref=first_near_recv.at[kind, step],
+            send_sem=near_send_sem.at[kind, step],
+            recv_sem=near_recv_sem.at[kind, step],
             device_id={"gx": neighbour},
             device_id_type=mesh_ids,
         )
 
-    def far_copy(send, recv, stage, step):
+    def first_far_copy(kind, step):
         return pltpu.make_async_remote_copy(
-            src_ref=send.at[step],
-            dst_ref=recv.at[step],
-            send_sem=far_send_sem.at[stage, step],
-            recv_sem=far_recv_sem.at[stage, step],
+            src_ref=first_far_send.at[kind, step],
+            dst_ref=first_far_recv.at[kind, step],
+            send_sem=far_send_sem.at[kind, step],
+            recv_sem=far_recv_sem.at[kind, step],
             device_id={"gx": column_at(step) * 2 + row},
             device_id_type=mesh_ids,
         )
@@ -320,33 +320,31 @@
         scale = power(-partial_exponent[core, target], width)
         return saturate(turn(memory_part[core, target], small_signs, norm) * scale)
 
+    terms = (memory_term, query_term)
+
     def first_near(step, carry):
         target = column_at(step) * 2 + 1 - row
-        first_near_send[step, 0] = query_term(target).astype(jnp.bfloat16)
-        first_near_send[step, 1] = memory_term(target).astype(jnp.bfloat16)
-        near_copy(first_near_send, first_near_recv, 0, step).start()
-        return carry
-
-    lax.fori_loop(0, columns_of, first_near, 0)
-
-    def first_joined(step):
-        target = column_at(step) * 2 + row
-        query, memory = query_term(target), memory_term(target)
-        near_copy(first_near_send, first_near_recv, 0, step).wait_recv()
-        query = query + first_near_recv[step, 0].astype(jnp.float32)
-        return query, memory + first_near_recv[step, 1].astype(jnp.float32)
+        for kind, term in enumerate(terms):
+            first_near_send[kind, step] = term(target).astype(jnp.bfloat16)
+            first_near_copy(kind, step).start()
+        return carry
+
+    def first_joined(kind, step):
+        term = terms[kind](column_at(step) * 2 + row)
+        first_near_copy(kind, step).wait_recv()
+        return term + first_near_recv[kind, step].astype(jnp.float32)
 
     def first_far(step, carry):
-        query, memory = first_joined(step)
-        first_far_send[step, 0] = query.astype(jnp.bfloat16)
-        first_far_send[step, 1] = memory.astype(jnp.bfloat16)
-        far_copy(first_far_send, first_far_recv, 0, step).start()
-        return carry
-
+        first_near(step + 1, 0)
+        for kind in range(2):
+            first_far_send[kind, step] = first_joined(kind, step).astype(jnp.bfloat16)
+            first_far_copy(kind, step).start()
+        return carry
+
+    first_near(0, 0)
     lax.fori_loop(0, columns_of - 1, first_far, 0)
-    query, memory = first_joined(columns_of - 1)
-    first_total[0] = query
-    first_total[1] = memory
+    for kind in range(2):
+        first_total[kind] = first_joined(kind, columns_of - 1)
 
     rows = lax.broadcasted_iota(jnp.int32, (length, length), 0)
     columns = lax.broadcasted_iota(jnp.int32, (length, length), 1)
@@ -354,21 +352,23 @@
     allowed = (rows >= columns) & (documents.T == documents)
     bias[...] = jnp.where(allowed, 0.0, -jnp.inf)
 
-    def first_sum(step, carry):
-        far_copy(first_far_send, first_far_recv, 0, step).wait_recv()
-        first_total[0] += first_far_recv[step, 0].astype(jnp.float32)
-        first_total[1] += first_far_recv[step, 1].astype(jnp.float32)
-        return carry
-
-    lax.fori_loop(0, columns_of - 1, first_sum, 0)
+    def first_sum(kind, step):
+        first_far_copy(kind, step).wait_recv()
+        first_total[kind] += first_far_recv[kind, step].astype(jnp.float32)
+
+    for step in range(columns_of - 1):
+        first_sum(0, step)
+        if step + 2 < columns_of:
+            first_sum(1, step)
 
     level_ratio = power(partial_exponent[core, me] - summed_exponent[core, me], width)
-    level = saturate(first_total[1] * level_ratio)
+    level = saturate(first_total[0] * level_ratio)
     memory = turn(level * power(summed_exponent[core, me], width), small_signs, norm)
     turned = memory * cosine_ref[...] + pltpu.roll(memory, width // 2, 1) * sine_ref[...]
     memory_pair[core] = jnp.where(core == 0, turned, memory).astype(jnp.bfloat16)
     pair_copy(memory_pair, 0).start()
-    query = turn(first_total[0] * power(query_exponent[me, 0], width), small_signs, norm)
+    first_sum(1, columns_of - 2)
+    query = turn(first_total[1] * power(query_exponent[me, 0], width), small_signs, norm)
     query = query * cosine_ref[...] + pltpu.roll(query, width // 2, 1) * sine_ref[...]
     query = query.astype(jnp.bfloat16)
     pair_copy(memory_pair, 0).wait_recv()
@@ -478,11 +478,13 @@
         out_copy(part).start()
 
     def drain_near(step, carry):
-        near_copy(first_near_send, first_near_recv, 0, step).wait_send()
+        first_near_copy(0, step).wait_send()
+        first_near_copy(1, step).wait_send()
         return carry
 
     def drain_far(step, carry):
-        far_copy(first_far_send, first_far_recv, 0, step).wait_send()
+        first_far_copy(0, step).wait_send()
+        first_far_copy(1, step).wait_send()
         return carry
 
     def drain_near_piece(piece, carry):
@@ -554,10 +556,10 @@
         out_specs=vmem,
         scratch_shapes=[
             pltpu.VMEM(output_weight.shape, bf16),
-            pltpu.VMEM((half, 2, length, width), bf16),
-            pltpu.VMEM((half, 2, length, width), bf16),
-            pltpu.VMEM((half - 1, 2, length, width), bf16),
-            pltpu.VMEM((half - 1, 2, length, width), bf16),
+            pltpu.VMEM((2, half, length, width), bf16),
+            pltpu.VMEM((2, half, length, width), bf16),
+            pltpu.VMEM((2, half - 1, length, width), bf16),
+            pltpu.VMEM((2, half - 1, length, width), bf16),
             pltpu.VMEM((2, length, width), bf16),
             pltpu.VMEM((2, length, width), bf16),
             pltpu.VMEM((half * parts, length, 2 * width), bf16),
@@ -568,10 +570,10 @@
             pltpu.VMEM((parts, length, 2 * width), jnp.float32),
             pltpu.VMEM((length, length), jnp.float32),
             pltpu.SemaphoreType.DMA,
-            pltpu.SemaphoreType.DMA((1, half)),
-            pltpu.SemaphoreType.DMA((1, half)),
-            pltpu.SemaphoreType.DMA((1, half - 1)),
-            pltpu.SemaphoreType.DMA((1, half - 1)),
+            pltpu.SemaphoreType.DMA((2, half)),
+            pltpu.SemaphoreType.DMA((2, half)),
+            pltpu.SemaphoreType.DMA((2, half - 1)),
+            pltpu.SemaphoreType.DMA((2, half - 1)),
             pltpu.SemaphoreType.DMA((2,)),
             pltpu.SemaphoreType.DMA((2,)),
             pltpu.SemaphoreType.DMA((half * parts,)),

time: 90.3 us -> 89 us (0.986)
  Pallas kernels: 79.2 us -> 77.7 us
    pallas_call x1, Pallas kernels: 79.2 us -> 77.7 us  [body(): pl.pallas_call(functools.partial(fused_kernel, count), out_shape=jax.Shap...]
where the time goes in v4:
time: 89 us; the launch traced here: 88.1 us
  Pallas kernels  77.7 us (87%)
  matrix products  5.96 us (7%)
  local copies, waits for them, and re-layouts  4.39 us (5%)
    pallas_call x1, Pallas kernels, body(): pl.pallas_call(functools.partial(fused_kernel, count), out_shape=jax.Shap...  77.7 us
    dot_general x1, matrix products, body(): jnp.einsum('sd,dpe->pse', tokens, query_weight[:, :, 0, :], preferred_ele...  3.58 us
    dot_general x1, matrix products, body(): jnp.einsum('sd,dcne->cnse', tokens, key_value_projection_weight, preferre...  2.38 us
    unnamed x23, local copies, waits for them, and re-layouts  2.34 us
    transpose x1, local copies, waits for them, and re-layouts, body(): return halves.transpose(1, 0, 2)  2.05 us

profile of v4, /device:TPU:0, one launch (start us, length us, event | category | flops | bytes accessed | tf_op | source)
XLA Modules:
  0.0 88.1 jit_solution(15453373909312911572)
XLA Ops:
  0.0 0.0 copy-start
  0.0 0.8 copy.18.query_exponent
  0.8 0.4 copy-done
  1.2 0.0 copy-start.10
  1.2 3.6 %fusion.7.query_part = f32[8,256,128]{2,1,0:T(8,128)S(1)} fusion(bf16[2048,8,128]{2,1,0:T(8,128)(2,1)} %bitcast.17, bf16[256,2048]{1,0:T(8,128)(2,1)S(1)} %copy-done), kind=kOutput, calls=%fused_computation.5 | convolution fusion | flops 1073741824 | bytes 6291456 | tf_op jit(solution)/shard_map/sd,dpe->pse/dot_general | solution.py:540
  4.8 1.1 %copy-done.10 = bf16[2048,2,8,128]{3,2,1,0:T(8,128)(2,1)S(1)} copy-done((bf16[2048,2,8,128]{3,2,1,0:T(8,128)(2,1)S(1)}, bf16[2048,2,8,128]{3,2,1,0:T(8,128)(2,1)}, u32[]{:S(2)}) %copy-start.10) | copy-done | bytes 8388632
  5.9 0.0 copy-start.1
  5.9 0.0 copy-start.2
  5.9 0.0 copy-start.3
  5.9 0.0 copy-start.4
  5.9 0.0 copy-start.5
  5.9 0.0 copy-start.6
  5.9 0.0 copy-start.7
  5.9 0.0 copy-start.8
  5.9 0.0 copy-start.9
  6.0 2.4 %fusion.4.memory_part = f32[2,8,256,128]{3,2,1,0:T(8,128)S(1)} fusion(bf16[2048,2,8,128]{3,2,1,0:T(8,128)(2,1)S(1)} %copy-done.10, bf16[256,2048]{1,0:T(8,128)(2,1)S(1)} %copy-done), kind=kOutput, calls=%fused_computation.4 | convolution fusion | flops 2147483648 | bytes 11534336 | tf_op jit(solution)/shard_map/sd,dcne->cnse/dot_general | solution.py:543
  8.3 0.0 copy-done.1
  8.4 0.0 copy-done.2
  8.4 0.0 copy-done.3
  8.4 0.0 copy-done.4
  8.4 0.0 copy-done.5
  8.4 0.0 copy-done.6
  8.4 0.0 copy-done.7
  8.4 0.0 copy-done.8
  8.4 0.0 copy-done.9
  8.4 77.7 %shard_map.127 = bf16[2,256,1024]{2,1,0:T(8,128)(2,1)S(1)} custom-call(f32[8,256,128]{2,1,0:T(8,128)S(1)} %fusion.7.query_part, f32[2,8,256,128]{3,2,1,0:T(8,128)S(1)} %fusion.4.memory_part, bf16[256,8192]{1,0:T(8,128)(2,1)S(1)} %copy-done.1, s32[1,256]{1,0:T(1,128)S(1)} %bitcast.16, s32[8,1]{1,0:T(8,128)S(1)} %copy.18.query_exponent, s32[2,8]{1,0:T(2,128)S(1)} %copy-done.6, ...), custom_call_target="tpu_custom_call" | custom-call | tf_op jit(solution)/shard_map/pallas_call | solution.py:552
  86.1 2.0 %copy.19 = bf16[256,2,1024]{2,1,0:T(2,128)(2,1)} copy(bf16[256,2,1024]{2,0,1:T(8,128)(2,1)S(1)} %bitcast.15) | data formatting | bytes 2097152 | tf_op jit(solution)/shard_map/transpose | solution.py:603
Async XLA Ops:
  0.0 1.2 %copy-start = (bf16[256,2048]{1,0:T(8,128)(2,1)S(1)}, bf16[256,2048]{1,0:T(8,128)(2,1)}, u32[]{:S(2)}) copy-start(bf16[256,2048]{1,0:T(8,128)(2,1)} %param.13) | copy-start | bytes 3145732
  1.2 4.6 %copy-start.10 = (bf16[2048,2,8,128]{3,2,1,0:T(8,128)(2,1)S(1)}, bf16[2048,2,8,128]{3,2,1,0:T(8,128)(2,1)}, u32[]{:S(2)}) copy-start(bf16[2048,2,8,128]{3,2,1,0:T(8,128)(2,1)} %param.15) | copy-start | bytes 25165828
  5.9 2.5 %copy-start.1 = (bf16[256,8192]{1,0:T(8,128)(2,1)S(1)}, bf16[256,8192]{1,0:T(8,128)(2,1)}, u32[]{:S(2)}) copy-start(bf16[256,8192]{1,0:T(8,128)(2,1)} %out_weight_hbm.1) | copy-start | bytes 12582916
  5.9 2.5 %copy-start.2 = (f32[256,128]{1,0:T(8,128)S(1)}, f32[256,128]{1,0:T(8,128)}, u32[]{:S(2)}) copy-start(f32[256,128]{1,0:T(8,128)} %constant.8.clone.sine_ref) | copy-start | bytes 393220
  5.9 2.5 %copy-start.3 = (f32[256,128]{1,0:T(8,128)S(1)}, f32[256,128]{1,0:T(8,128)}, u32[]{:S(2)}) copy-start(f32[256,128]{1,0:T(8,128)} %constant.7.clone.cosine_ref) | copy-start | bytes 393220
  5.9 2.5 %copy-start.4 = (bf16[256,256]{1,0:T(8,128)(2,1)S(1)}, bf16[256,256]{1,0:T(8,128)(2,1)}, u32[]{:S(2)}) copy-start(bf16[256,256]{1,0:T(8,128)(2,1)} %constant.6.clone.sign_ref) | copy-start | bytes 393220
  5.9 2.5 %copy-start.5 = (s32[256]{0:T(256)S(1)}, s32[256]{0:T(256)}, u32[]{:S(2)}) copy-start(s32[256]{0:T(256)} %param.17) | copy-start | bytes 3076
  5.9 2.5 %copy-start.6 = (s32[2,8]{1,0:T(2,128)S(1)}, s32[2,8]{1,0:T(2,128)}, u32[]{:S(2)}) copy-start(s32[2,8]{1,0:T(2,128)} %partial_exponent.1) | copy-start | bytes 196
  5.9 2.5 %copy-start.7 = (s32[2,8]{1,0:T(2,128)S(1)}, s32[2,8]{1,0:T(2,128)}, u32[]{:S(2)}) copy-start(s32[2,8]{1,0:T(2,128)} %summed_exponent.1) | copy-start | bytes 196
  5.9 2.5 %copy-start.8 = (s32[2,8]{1,0:T(2,128)S(1)}, s32[2,8]{1,0:T(2,128)}, u32[]{:S(2)}) copy-start(s32[2,8]{1,0:T(2,128)} %relevel.1) | copy-start | bytes 196
  5.9 2.5 %copy-start.9 = (s32[1,64]{1,0:T(1,128)S(1)}, s32[1,64]{1,0:T(1,128)}, u32[]{:S(2)}) copy-start(s32[1,64]{1,0:T(1,128)} %out_exponent.1) | copy-start | bytes 772

commit v5 on v4

--- a/solution.py
+++ b/solution.py
@@ -313,7 +313,7 @@
         )
 
     def query_term(target):
-        scale = power(-query_exponent[target, 0], width)
+        scale = power(-query_exponent[0, target], width)
         return saturate(turn(query_part[target], small_signs, norm) * scale)
 
     def memory_term(target):
@@ -368,7 +368,7 @@
     memory_pair[core] = jnp.where(core == 0, turned, memory).astype(jnp.bfloat16)
     pair_copy(memory_pair, 0).start()
     first_sum(1, columns_of - 2)
-    query = turn(first_total[1] * power(query_exponent[me, 0], width), small_signs, norm)
+    query = turn(first_total[1] * power(query_exponent[0, me], width), small_signs, norm)
     query = query * cosine_ref[...] + pltpu.roll(query, width // 2, 1) * sine_ref[...]
     query = query.astype(jnp.bfloat16)
     pair_copy(memory_pair, 0).wait_recv()
@@ -400,7 +400,7 @@
         return saturate(turn(product, sign_ref[...], norm) * scale)
 
     parts = span // chunk
-    ahead = min(3, parts)
+    ahead = parts
     near_total, far_total = columns_of * parts, (columns_of - 1) * parts
 
     def piece_copy(kind, piece):
@@ -591,7 +591,7 @@
         memory_part,
         output_weight,
         document_ids[None, :],
-        query_exponent,
+        query_exponent.T,
         key_value_partial_exponents,
         key_value_summed_exponents,
         output_exponent,

time: 89 us -> 88.9 us (level)
    unnamed x23 -> x24, local copies, waits for them, and re-layouts: 2.34 us -> 2.33 us
where the time goes in v5:
time: 88.9 us; the launch traced here: 88.1 us
  Pallas kernels  77.6 us (87%)
  matrix products  5.95 us (7%)
  local copies, waits for them, and re-layouts  4.38 us (5%)
    pallas_call x1, Pallas kernels, body(): pl.pallas_call(functools.partial(fused_kernel, count), out_shape=jax.Shap...  77.6 us
    dot_general x1, matrix products, body(): jnp.einsum('sd,dpe->pse', tokens, query_weight[:, :, 0, :], preferred_ele...  3.58 us
    dot_general x1, matrix products, body(): jnp.einsum('sd,dcne->cnse', tokens, key_value_projection_weight, preferre...  2.38 us
    unnamed x24, local copies, waits for them, and re-layouts  2.33 us
    transpose x1, local copies, waits for them, and re-layouts, body(): return halves.transpose(1, 0, 2)  2.05 us

profile of v5, /device:TPU:0, one launch (start us, length us, event | category | flops | bytes accessed | tf_op | source)
XLA Modules:
  0.0 88.1 jit_solution(13989150320359794422)
XLA Ops:
  0.0 0.0 copy-start
  0.0 1.2 %copy-done = bf16[256,2048]{1,0:T(8,128)(2,1)S(1)} copy-done((bf16[256,2048]{1,0:T(8,128)(2,1)S(1)}, bf16[256,2048]{1,0:T(8,128)(2,1)}, u32[]{:S(2)}) %copy-start) | copy-done | bytes 1048600
  1.2 0.0 copy-start.11
  1.2 3.6 %fusion.7.query_part = f32[8,256,128]{2,1,0:T(8,128)S(1)} fusion(bf16[2048,8,128]{2,1,0:T(8,128)(2,1)} %bitcast.19, bf16[256,2048]{1,0:T(8,128)(2,1)S(1)} %copy-done), kind=kOutput, calls=%fused_computation.5 | convolution fusion | flops 1073741824 | bytes 6291456 | tf_op jit(solution)/shard_map/sd,dpe->pse/dot_general | solution.py:540
  4.8 1.1 %copy-done.11 = bf16[2048,2,8,128]{3,2,1,0:T(8,128)(2,1)S(1)} copy-done((bf16[2048,2,8,128]{3,2,1,0:T(8,128)(2,1)S(1)}, bf16[2048,2,8,128]{3,2,1,0:T(8,128)(2,1)}, u32[]{:S(2)}) %copy-start.11) | copy-done | bytes 8388632
  5.9 0.0 copy-start.1
  5.9 0.0 copy-start.2
  5.9 0.0 copy-start.3
  5.9 0.0 copy-start.4
  5.9 0.0 copy-start.5
  5.9 0.0 copy-start.6
  5.9 0.0 copy-start.7
  5.9 0.0 copy-start.8
  5.9 0.0 copy-start.9
  5.9 0.0 copy-start.10
  6.0 2.4 %fusion.4.memory_part = f32[2,8,256,128]{3,2,1,0:T(8,128)S(1)} fusion(bf16[2048,2,8,128]{3,2,1,0:T(8,128)(2,1)S(1)} %copy-done.11, bf16[256,2048]{1,0:T(8,128)(2,1)S(1)} %copy-done), kind=kOutput, calls=%fused_computation.4 | convolution fusion | flops 2147483648 | bytes 11534336 | tf_op jit(solution)/shard_map/sd,dcne->cnse/dot_general | solution.py:543
  8.3 0.0 copy-done.1
  8.3 0.0 copy-done.2
  8.4 0.0 copy-done.3
  8.4 0.0 copy-done.4
  8.4 0.0 copy-done.5
  8.4 0.0 copy-done.6
  8.4 0.0 copy-done.7
  8.4 0.0 copy-done.8
  8.4 0.0 copy-done.9
  8.4 0.0 copy-done.10
  8.4 77.6 %shard_map.127 = bf16[2,256,1024]{2,1,0:T(8,128)(2,1)S(1)} custom-call(f32[8,256,128]{2,1,0:T(8,128)S(1)} %fusion.7.query_part, f32[2,8,256,128]{3,2,1,0:T(8,128)S(1)} %fusion.4.memory_part, bf16[256,8192]{1,0:T(8,128)(2,1)S(1)} %copy-done.1, s32[1,256]{1,0:T(1,128)S(1)} %bitcast.17, s32[1,8]{1,0:T(1,128)S(1)} %bitcast.18, s32[2,8]{1,0:T(2,128)S(1)} %copy-done.6, ...), custom_call_target="tpu_custom_call" | custom-call | tf_op jit(solution)/shard_map/pallas_call | solution.py:552
  86.0 2.0 %copy.18 = bf16[256,2,1024]{2,1,0:T(2,128)(2,1)} copy(bf16[256,2,1024]{2,0,1:T(8,128)(2,1)S(1)} %bitcast.16) | data formatting | bytes 2097152 | tf_op jit(solution)/shard_map/transpose | solution.py:603
Async XLA Ops:
  0.0 1.2 %copy-start = (bf16[256,2048]{1,0:T(8,128)(2,1)S(1)}, bf16[256,2048]{1,0:T(8,128)(2,1)}, u32[]{:S(2)}) copy-start(bf16[256,2048]{1,0:T(8,128)(2,1)} %param.13) | copy-start | bytes 3145732
  1.2 4.6 %copy-start.11 = (bf16[2048,2,8,128]{3,2,1,0:T(8,128)(2,1)S(1)}, bf16[2048,2,8,128]{3,2,1,0:T(8,128)(2,1)}, u32[]{:S(2)}) copy-start(bf16[2048,2,8,128]{3,2,1,0:T(8,128)(2,1)} %param.15) | copy-start | bytes 25165828
  5.9 2.5 %copy-start.1 = (bf16[256,8192]{1,0:T(8,128)(2,1)S(1)}, bf16[256,8192]{1,0:T(8,128)(2,1)}, u32[]{:S(2)}) copy-start(bf16[256,8192]{1,0:T(8,128)(2,1)} %out_weight_hbm.1) | copy-start | bytes 12582916
  5.9 2.5 %copy-start.2 = (f32[256,128]{1,0:T(8,128)S(1)}, f32[256,128]{1,0:T(8,128)}, u32[]{:S(2)}) copy-start(f32[256,128]{1,0:T(8,128)} %constant.8.clone.sine_ref) | copy-start | bytes 393220
  5.9 2.5 %copy-start.3 = (f32[256,128]{1,0:T(8,128)S(1)}, f32[256,128]{1,0:T(8,128)}, u32[]{:S(2)}) copy-start(f32[256,128]{1,0:T(8,128)} %constant.7.clone.cosine_ref) | copy-start | bytes 393220
  5.9 2.5 %copy-start.4 = (bf16[256,256]{1,0:T(8,128)(2,1)S(1)}, bf16[256,256]{1,0:T(8,128)(2,1)}, u32[]{:S(2)}) copy-start(bf16[256,256]{1,0:T(8,128)(2,1)} %constant.6.clone.sign_ref) | copy-start | bytes 393220
  5.9 2.5 %copy-start.5 = (s32[256]{0:T(256)S(1)}, s32[256]{0:T(256)}, u32[]{:S(2)}) copy-start(s32[256]{0:T(256)} %param.17) | copy-start | bytes 3076
  5.9 2.5 %copy-start.6 = (s32[2,8]{1,0:T(2,128)S(1)}, s32[2,8]{1,0:T(2,128)}, u32[]{:S(2)}) copy-start(s32[2,8]{1,0:T(2,128)} %partial_exponent.1) | copy-start | bytes 196
  5.9 2.5 %copy-start.7 = (s32[2,8]{1,0:T(2,128)S(1)}, s32[2,8]{1,0:T(2,128)}, u32[]{:S(2)}) copy-start(s32[2,8]{1,0:T(2,128)} %summed_exponent.1) | copy-start | bytes 196
  5.9 2.5 %copy-start.8 = (s32[2,8]{1,0:T(2,128)S(1)}, s32[2,8]{1,0:T(2,128)}, u32[]{:S(2)}) copy-start(s32[2,8]{1,0:T(2,128)} %relevel.1) | copy-start | bytes 196
  5.9 2.5 %copy-start.9 = (s32[8,1]{0,1:T(1,128)S(1)}, s32[8,1]{0,1:T(1,128)}, u32[]{:S(2)}) copy-start(s32[8,1]{0,1:T(1,128)} %param.18) | copy-start | bytes 100
  5.9 2.5 %copy-start.10 = (s32[1,64]{1,0:T(1,128)S(1)}, s32[1,64]{1,0:T(1,128)}, u32[]{:S(2)}) copy-start(s32[1,64]{1,0:T(1,128)} %out_exponent.1) | copy-start | bytes 772

commit v6 on v5

--- a/solution.py
+++ b/solution.py
@@ -266,6 +266,8 @@
     load.start()
 
     def column_at(step):
+        if columns_of == 4:
+            return lax.rem(column + 2 + 3 * step + 3 * ((step * (step - 1)) // 2), 4)
         return lax.rem(column + 1 + step, columns_of)
 
     barrier = pltpu.get_barrier_semaphore()

time: 88.9 us -> 87.9 us (0.989)
  no operation moved by 1% of the time
where the time goes in v6:
time: 87.9 us; the launch traced here: 87.8 us
  Pallas kernels  77.3 us (88%)
  matrix products  5.95 us (7%)
  local copies, waits for them, and re-layouts  4.38 us (5%)
    pallas_call x1, Pallas kernels, body(): pl.pallas_call(functools.partial(fused_kernel, count), out_shape=jax.Shap...  77.3 us
    dot_general x1, matrix products, body(): jnp.einsum('sd,dpe->pse', tokens, query_weight[:, :, 0, :], preferred_ele...  3.58 us
    dot_general x1, matrix products, body(): jnp.einsum('sd,dcne->cnse', tokens, key_value_projection_weight, preferre...  2.38 us
    unnamed x24, local copies, waits for them, and re-layouts  2.33 us
    transpose x1, local copies, waits for them, and re-layouts, body(): return halves.transpose(1, 0, 2)  2.05 us

profile of v6, /device:TPU:0, one launch (start us, length us, event | category | flops | bytes accessed | tf_op | source)
XLA Modules:
  0.0 87.8 jit_solution(9693718838353356374)
XLA Ops:
  0.0 0.0 copy-start
  0.0 1.2 %copy-done = bf16[256,2048]{1,0:T(8,128)(2,1)S(1)} copy-done((bf16[256,2048]{1,0:T(8,128)(2,1)S(1)}, bf16[256,2048]{1,0:T(8,128)(2,1)}, u32[]{:S(2)}) %copy-start) | copy-done | bytes 1048600
  1.2 0.0 copy-start.11
  1.2 3.6 %fusion.7.query_part = f32[8,256,128]{2,1,0:T(8,128)S(1)} fusion(bf16[2048,8,128]{2,1,0:T(8,128)(2,1)} %bitcast.19, bf16[256,2048]{1,0:T(8,128)(2,1)S(1)} %copy-done), kind=kOutput, calls=%fused_computation.5 | convolution fusion | flops 1073741824 | bytes 6291456 | tf_op jit(solution)/shard_map/sd,dpe->pse/dot_general | solution.py:542
  4.8 1.1 %copy-done.11 = bf16[2048,2,8,128]{3,2,1,0:T(8,128)(2,1)S(1)} copy-done((bf16[2048,2,8,128]{3,2,1,0:T(8,128)(2,1)S(1)}, bf16[2048,2,8,128]{3,2,1,0:T(8,128)(2,1)}, u32[]{:S(2)}) %copy-start.11) | copy-done | bytes 8388632
  5.9 0.0 copy-start.1
  5.9 0.0 copy-start.2
  5.9 0.0 copy-start.3
  5.9 0.0 copy-start.4
  5.9 0.0 copy-start.5
  5.9 0.0 copy-start.6
  5.9 0.0 copy-start.7
  5.9 0.0 copy-start.8
  5.9 0.0 copy-start.9
  5.9 0.0 copy-start.10
  6.0 2.4 %fusion.4.memory_part = f32[2,8,256,128]{3,2,1,0:T(8,128)S(1)} fusion(bf16[2048,2,8,128]{3,2,1,0:T(8,128)(2,1)S(1)} %copy-done.11, bf16[256,2048]{1,0:T(8,128)(2,1)S(1)} %copy-done), kind=kOutput, calls=%fused_computation.4 | convolution fusion | flops 2147483648 | bytes 11534336 | tf_op jit(solution)/shard_map/sd,dcne->cnse/dot_general | solution.py:545
  8.3 0.0 copy-done.1
  8.3 0.0 copy-done.2
  8.4 0.0 copy-done.3
  8.4 0.0 copy-done.4
  8.4 0.0 copy-done.5
  8.4 0.0 copy-done.6
  8.4 0.0 copy-done.7
  8.4 0.0 copy-done.8
  8.4 0.0 copy-done.9
  8.4 0.0 copy-done.10
  8.4 77.3 %shard_map.127 = bf16[2,256,1024]{2,1,0:T(8,128)(2,1)S(1)} custom-call(f32[8,256,128]{2,1,0:T(8,128)S(1)} %fusion.7.query_part, f32[2,8,256,128]{3,2,1,0:T(8,128)S(1)} %fusion.4.memory_part, bf16[256,8192]{1,0:T(8,128)(2,1)S(1)} %copy-done.1, s32[1,256]{1,0:T(1,128)S(1)} %bitcast.17, s32[1,8]{1,0:T(1,128)S(1)} %bitcast.18, s32[2,8]{1,0:T(2,128)S(1)} %copy-done.6, ...), custom_call_target="tpu_custom_call" | custom-call | tf_op jit(solution)/shard_map/pallas_call | solution.py:554
  85.7 2.0 %copy.18 = bf16[256,2,1024]{2,1,0:T(2,128)(2,1)} copy(bf16[256,2,1024]{2,0,1:T(8,128)(2,1)S(1)} %bitcast.16) | data formatting | bytes 2097152 | tf_op jit(solution)/shard_map/transpose | solution.py:605
Async XLA Ops:
  0.0 1.2 %copy-start = (bf16[256,2048]{1,0:T(8,128)(2,1)S(1)}, bf16[256,2048]{1,0:T(8,128)(2,1)}, u32[]{:S(2)}) copy-start(bf16[256,2048]{1,0:T(8,128)(2,1)} %param.13) | copy-start | bytes 3145732
  1.2 4.6 %copy-start.11 = (bf16[2048,2,8,128]{3,2,1,0:T(8,128)(2,1)S(1)}, bf16[2048,2,8,128]{3,2,1,0:T(8,128)(2,1)}, u32[]{:S(2)}) copy-start(bf16[2048,2,8,128]{3,2,1,0:T(8,128)(2,1)} %param.15) | copy-start | bytes 25165828
  5.9 2.5 %copy-start.1 = (bf16[256,8192]{1,0:T(8,128)(2,1)S(1)}, bf16[256,8192]{1,0:T(8,128)(2,1)}, u32[]{:S(2)}) copy-start(bf16[256,8192]{1,0:T(8,128)(2,1)} %out_weight_hbm.1) | copy-start | bytes 12582916
  5.9 2.5 %copy-start.2 = (f32[256,128]{1,0:T(8,128)S(1)}, f32[256,128]{1,0:T(8,128)}, u32[]{:S(2)}) copy-start(f32[256,128]{1,0:T(8,128)} %constant.8.clone.sine_ref) | copy-start | bytes 393220
  5.9 2.5 %copy-start.3 = (f32[256,128]{1,0:T(8,128)S(1)}, f32[256,128]{1,0:T(8,128)}, u32[]{:S(2)}) copy-start(f32[256,128]{1,0:T(8,128)} %constant.7.clone.cosine_ref) | copy-start | bytes 393220
  5.9 2.5 %copy-start.4 = (bf16[256,256]{1,0:T(8,128)(2,1)S(1)}, bf16[256,256]{1,0:T(8,128)(2,1)}, u32[]{:S(2)}) copy-start(bf16[256,256]{1,0:T(8,128)(2,1)} %constant.6.clone.sign_ref) | copy-start | bytes 393220
  5.9 2.5 %copy-start.5 = (s32[256]{0:T(256)S(1)}, s32[256]{0:T(256)}, u32[]{:S(2)}) copy-start(s32[256]{0:T(256)} %param.17) | copy-start | bytes 3076
  5.9 2.5 %copy-start.6 = (s32[2,8]{1,0:T(2,128)S(1)}, s32[2,8]{1,0:T(2,128)}, u32[]{:S(2)}) copy-start(s32[2,8]{1,0:T(2,128)} %partial_exponent.1) | copy-start | bytes 196
  5.9 2.5 %copy-start.7 = (s32[2,8]{1,0:T(2,128)S(1)}, s32[2,8]{1,0:T(2,128)}, u32[]{:S(2)}) copy-start(s32[2,8]{1,0:T(2,128)} %summed_exponent.1) | copy-start | bytes 196
  5.9 2.5 %copy-start.8 = (s32[2,8]{1,0:T(2,128)S(1)}, s32[2,8]{1,0:T(2,128)}, u32[]{:S(2)}) copy-start(s32[2,8]{1,0:T(2,128)} %relevel.1) | copy-start | bytes 196
  5.9 2.5 %copy-start.9 = (s32[8,1]{0,1:T(1,128)S(1)}, s32[8,1]{0,1:T(1,128)}, u32[]{:S(2)}) copy-start(s32[8,1]{0,1:T(1,128)} %param.18) | copy-start | bytes 100
  5.9 2.5 %copy-start.10 = (s32[1,64]{1,0:T(1,128)S(1)}, s32[1,64]{1,0:T(1,128)}, u32[]{:S(2)}) copy-start(s32[1,64]{1,0:T(1,128)} %out_exponent.1) | copy-start | bytes 772
